TPU v7x, 512 devices: a whole 4x4x16 slice. The times are simulated.
512 devices in a mesh: group: 16 (over y_hi, x, core), dev: 32 (over z, y_lo).
Axes of the slice: x: 4, y: 4 (y_hi: 2, y_lo: 2; y = y_hi * 2 + y_lo), z: 16, core: 2. Of those that a mesh axis runs over, the one named last changes fastest.
Arguments:
- user_feat: bfloat16 [65536, 1024], P(('group', 'dev')), may hold values from -6 to 6
- item_feat: bfloat16 [65536, 1024], P(('group', 'dev')), may hold values from -6 to 6
- item_ids: int32 [65536], P(('group', 'dev')), may hold values from 0 to 1048575
- corpus_feat: bfloat16 [131072, 1024], P(('group', 'dev')), may hold values from -6 to 6
- neg_owner: int32 [262144, 1], P(('group', 'dev')), may hold values from 0 to 31; in each aligned block of 512 rows (0 to 511, 512 to 1023, ...) at most 48 rows name the same one
- neg_row: int32 [262144], P(('group', 'dev')), may hold values from 0 to 255
- user_weight: bfloat16 [1024, 256], replicated, may hold values from -0.1875 to 0.1875
- item_weight: bfloat16 [1024, 256], replicated, may hold values from -0.1875 to 0.1875
Outputs:
- loss: float32 [65536], P(('group', 'dev'))
- grad_user: float32 [1024, 256], replicated
- grad_item: float32 [1024, 256], replicated
Inputs may be any that keep to these rules, and one draw needn't show every extreme that they name: `neg_owner`: among the 512 samples of one device, no owner is named more than 48 times, a bound that some block reaches.
All inputs are finite; a program needn't handle non-finite values.
Results may differ from a plain program's by a relative error of at most 0.00075.
The roundings to bfloat16 on the way count: a program that leaves them out, or rounds other values in their place, can miss the bound.
Values may be sent and summed in bfloat16 or wider, within the bound.
A program may use at most 64 MiB of HBM per device.

v0:
```python
import jax
import jax.numpy as jnp
from jax import lax
from jax.sharding import PartitionSpec as P

sharpen = 20.0
epsilon = 1e-06


def project(features, weight):
    hidden = jnp.dot(features, weight, preferred_element_type=jnp.float32)
    inverse = lax.rsqrt(jnp.sum(hidden * hidden, axis=-1, keepdims=True) + epsilon)
    return (hidden * inverse, inverse)


def unnormalize(unit, inverse, upstream):
    along = jnp.sum(unit * upstream, axis=-1, keepdims=True)
    return ((upstream - unit * along) * inverse).astype(jnp.bfloat16)


def contract(left, right, left_dim, right_dim):
    return lax.dot_general(
        left, right, (((left_dim,), (right_dim,)), ((), ())), preferred_element_type=jnp.float32
    )


def local(
    user_feat, item_feat, item_ids, corpus_feat, neg_owner, neg_row, user_weight, item_weight
):
    tok_rows = user_feat.shape[0]
    owner_count = lax.axis_size("dev")
    sample_count = neg_row.shape[0]
    capacity = 3 * sample_count // owner_count
    width = user_weight.shape[1]
    owned_rows = corpus_feat.shape[0]
    factor = sharpen / tok_rows
    user_unit, user_inv = project(user_feat, user_weight)
    user_low = user_unit.astype(jnp.bfloat16)
    item_unit, item_inv = project(item_feat, item_weight)
    item_low = item_unit.astype(jnp.bfloat16)
    cycle_items, cycle_ids = (
        lax.all_gather(item_low, "group", axis=0, tiled=True),
        lax.all_gather(item_ids, "group", axis=0, tiled=True),
    )
    owners = neg_owner[:, 0]
    owner_hot = (owners[:, None] == jnp.arange(owner_count, dtype=jnp.int32)[None, :]).astype(
        jnp.int32
    )
    earlier = jnp.cumsum(owner_hot, axis=0) - owner_hot
    slot = owners * capacity + jnp.sum(earlier * owner_hot, axis=1)
    wanted = jnp.full((owner_count * capacity,), -1, jnp.int32).at[slot].set(neg_row)
    requests = lax.all_to_all(
        wanted.reshape(owner_count, capacity), "dev", split_axis=0, concat_axis=0, tiled=True
    ).reshape(-1)
    valid = requests >= 0
    safe_rows = jnp.where(valid, requests, 0)
    corpus_unit, corpus_inv = project(corpus_feat, item_weight)
    reply = corpus_unit.astype(jnp.bfloat16)[safe_rows].reshape(owner_count, capacity, width)
    arrived = lax.all_to_all(reply, "dev", split_axis=0, concat_axis=0, tiled=True).reshape(
        owner_count * capacity, width
    )
    sample_low = arrived[slot]
    cycle_logit = sharpen * contract(user_low, cycle_items, 1, 1)
    sample_logit = sharpen * contract(user_low, sample_low, 1, 1)
    columns = jnp.arange(cycle_ids.shape[0], dtype=jnp.int32)
    here = lax.axis_index("group")
    own_column = here * tok_rows + jnp.arange(tok_rows, dtype=jnp.int32)
    diagonal = columns[None, :] == own_column[:, None]
    keep = jnp.logical_not((cycle_ids[None, :] == item_ids[:, None]) & jnp.logical_not(diagonal))
    cycle_exp = jnp.where(keep, jnp.exp(cycle_logit), jnp.float32(0.0))
    sample_exp = jnp.exp(sample_logit)
    total = jnp.sum(cycle_exp, axis=1) + jnp.sum(sample_exp, axis=1)
    own_logit = jnp.sum(jnp.where(diagonal, cycle_logit, jnp.float32(0.0)), axis=1)
    loss = jnp.log(total) - own_logit
    cycle_grad = ((cycle_exp / total[:, None] - diagonal.astype(jnp.float32)) * factor).astype(
        jnp.bfloat16
    )
    sample_grad = (sample_exp / total[:, None] * factor).astype(jnp.bfloat16)
    user_up = jnp.dot(cycle_grad, cycle_items, preferred_element_type=jnp.float32) + jnp.dot(
        sample_grad, sample_low, preferred_element_type=jnp.float32
    )
    item_up = lax.psum_scatter(
        contract(cycle_grad, user_low, 0, 0), "group", scatter_dimension=0, tiled=True
    )
    sample_up = contract(sample_grad, user_low, 0, 0)
    placed = jnp.zeros((owner_count * capacity, width), jnp.float32).at[slot].set(sample_up)
    returned = lax.all_to_all(
        placed.reshape(owner_count, capacity, width), "dev", split_axis=0, concat_axis=0, tiled=True
    ).reshape(owner_count * capacity, width)
    slot_back = unnormalize(corpus_unit[safe_rows], corpus_inv[safe_rows], returned)
    owner_table = (
        (jnp.arange(owned_rows, dtype=jnp.int32)[:, None] == requests[None, :]) & valid[None, :]
    ).astype(jnp.bfloat16)
    owned_back = jnp.dot(owner_table, slot_back, preferred_element_type=jnp.float32)
    corpus_grad = lax.dot_general(
        corpus_feat.astype(jnp.float32),
        owned_back,
        (((0,), (0,)), ((), ())),
        precision=lax.Precision.HIGHEST,
        preferred_element_type=jnp.float32,
    )
    user_back = unnormalize(user_unit, user_inv, user_up)
    item_back = unnormalize(item_unit, item_inv, item_up)
    grad_user = contract(user_feat, user_back, 0, 0)
    grad_item = contract(item_feat, item_back, 0, 0) + corpus_grad
    grad_user, grad_item = lax.psum((grad_user, grad_item), ("group", "dev"))
    return (loss, grad_user, grad_item)


def solution(mesh):
    return jax.shard_map(
        local,
        mesh=mesh,
        in_specs=(
            P(("group", "dev"), None),
            P(("group", "dev"), None),
            P(("group", "dev")),
            P(("group", "dev"), None),
            P(("group", "dev"), None),
            P(("group", "dev")),
            P(),
            P(),
        ),
        out_specs=(P(("group", "dev")), P(), P()),
        check_vma=False,
    )
```

profile of v0, /device:TPU:1, one launch (start us, length us, event | category | flops | bytes accessed | tf_op | source)
XLA Modules:
  0.0 739.5 jit_solution(13646766417607443083)
XLA Ops:
  7.2 0.7 fusion.22
  7.9 1.2 reduce-window.6
  9.3 0.8 fusion.17
  10.8 2.6 scatter_custom_fusion
  13.4 0.7 all_to_all.12
  14.1 17.0 %all-to-all-start = ((s32[32,1,48]{2,1,0:T(1,128)}), s32[32,1,48]{2,1,0:T(1,128)S(1)}, u32[]{:S(2)}, u32[]{:S(2)}) async-start(s32[32,1,48]{2,1,0:T(1,128)} %all_to_all.12), calls=%async_computation | async-start | bytes 32768 | tf_op jit(solution)/shard_map/all_to_all | solution.py:52
  31.2 1.4 multiply_reduce_fusion.1
  32.8 10.4 %all-to-all-done = s32[32,1,48]{2,1,0:T(1,128)S(1)} async-done(((s32[32,1,48]{2,1,0:T(1,128)}), s32[32,1,48]{2,1,0:T(1,128)S(1)}, u32[]{:S(2)}, u32[]{:S(2)}) %all-to-all-start) | async-done | bytes 6176 | tf_op jit(solution)/shard_map/all_to_all | solution.py:52
  44.5 5.4 gather_fusion
  49.9 4.1 all-to-all-start.1
  54.4 0.7 multiply_convert_fusion.4
  55.1 25.8 %all-gather = s32[16,1,128]{2,1,0:T(1,128)S(1)} all-gather(s32[1,1,128]{2,1,0:T(1,128)S(1)} %bitcast.75), channel_id=1, replica_groups=mesh['group'=16,'dev'=32] {'group'}, dimensions={0}, use_global_device_ids=true | all-gather | bytes 8704 | tf_op jit(solution)/shard_map/all_gather | solution.py:43
  81.4 40.5 %all-gather.3.cloned.1.call-done = bf16[2048,256]{1,0:T(8,128)(2,1)} async-done(((bf16[128,256]{1,0:T(8,128)(2,1)}), bf16[2048,256]{1,0:T(8,128)(2,1)}) %all-gather.3.cloned.1.call-update) | async-done | bytes 1048592 | tf_op jit(solution)/shard_map/all_gather | solution.py:42
  121.9 2.9 fusion.13
  124.8 1.9 gather_fusion.1
  128.0 3.5 scatter_custom_fusion.1
  131.5 12.3 %all-to-all-start.2 = ((f32[32,48,256]{2,1,0:T(8,128)}), f32[32,48,256]{2,1,0:T(8,128)S(1)}, u32[]{:S(2)}, u32[]{:S(2)}) async-start(f32[32,48,256]{2,1,0:T(8,128)} %bitcast.65), calls=%async_computation.3 | async-start | bytes 3145728 | tf_op jit(solution)/shard_map/all_to_all | solution.py:87
  143.8 2.1 multiply_convert_fusion
  145.9 1.8 fusion.30
  148.1 12.8 %gather_fusion.3 = f32[1536]{0:T(1024)} fusion(f32[256]{0:T(256)S(1)} %add_rsqrt_fusion, s32[2048]{0:T(1024)S(1)} %pad_clamp_fusion), kind=kCustom, calls=%fused_computation.3 | custom fusion | bytes 18432 | tf_op jit(solution)/shard_map/gather | solution.py:90
  161.0 4.6 gather_fusion.2
  166.3 1.6 fusion.29
  168.2 1.4 convolution_bitcast_fusion
  169.6 73.5 %reduce-scatter.2.cloned.1.call-done = f32[128,256]{1,0:T(8,128)} async-done(((f32[2048,256]{1,0:T(8,128)}), f32[128,256]{1,0:T(8,128)}) %reduce-scatter.2.cloned.1.call-update) | async-done | bytes 131088 | tf_op jit(solution)/shard_map/reduce_scatter | solution.py:82
  243.1 1.1 multiply_reduce_fusion.2
  244.2 1.3 fusion.14
  245.5 1.8 multiply_reduce_fusion
  247.4 2.1 fusion.1
  249.9 1.6 fusion.5
  251.6 477.5 %all-reduce.3.cloned.1.call-done = (f32[1024,256]{0,1:T(8,128)}, f32[1024,256]{0,1:T(8,128)}) async-done(((f32[1024,256]{0,1:T(8,128)}, f32[1024,256]{0,1:T(8,128)}), (f32[1024,256]{0,1:T(8,128)}, f32[1024,256]{0,1:T(8,128)})) %all-reduce.3.cloned.1.call-update) | async-done | bytes 2097168 | tf_op jit(solution)/shard_map/psum | solution.py:106
  729.1 2.6 copy.23
  731.7 1.3 copy.24
  (74 shorter events, 6.4 us)
Async XLA Ops:
  7.2 24.0 %copy-start = (bf16[256,1024]{1,0:T(8,128)(2,1)S(1)}, bf16[256,1024]{1,0:T(8,128)(2,1)}, u32[]{:S(2)}) copy-start(bf16[256,1024]{1,0:T(8,128)(2,1)} %param.11) | copy-start | bytes 1572868
  14.1 29.0 %all-to-all-start = ((s32[32,1,48]{2,1,0:T(1,128)}), s32[32,1,48]{2,1,0:T(1,128)S(1)}, u32[]{:S(2)}, u32[]{:S(2)}) async-start(s32[32,1,48]{2,1,0:T(1,128)} %all_to_all.12), calls=%async_computation | async-start | bytes 32768 | tf_op jit(solution)/shard_map/all_to_all | solution.py:52
  49.9 4.1 copy-start.1
  49.9 4.1 copy-start.5
  49.9 5.2 copy-start.13
  49.9 31.1 %copy-start.3 = (bf16[128,1024]{1,0:T(8,128)(2,1)S(1)}, bf16[128,1024]{1,0:T(8,128)(2,1)}, u32[]{:S(2)}) copy-start(bf16[128,1024]{1,0:T(8,128)(2,1)} %param.8) | copy-start | bytes 786436
  49.9 31.1 %copy-start.9 = (bf16[1024,256]{1,0:T(8,128)(2,1)S(1)}, bf16[1024,256]{1,0:T(8,128)(2,1)}, u32[]{:S(2)}) copy-start(bf16[1024,256]{1,0:T(8,128)(2,1)} %param.14) | copy-start | bytes 1572868
  49.9 74.9 %all-to-all-start.1 = ((bf16[32,48,256]{2,1,0:T(8,128)(2,1)}), bf16[32,48,256]{2,1,0:T(8,128)(2,1)S(1)}, u32[]{:S(2)}, u32[]{:S(2)}) async-start(bf16[32,48,256]{2,1,0:T(8,128)(2,1)} %bitcast.7), calls=%async_computation.1 | async-start | bytes 1572864 | tf_op jit(solution)/shard_map/all_to_all | solution.py:59
  54.0 67.9 %all-gather.3.cloned.1.call-start = ((), (), s32[]{:S(2)}) async-start(), calls=%async_computation.4 | async-start | bytes 1114112 | tf_op jit(solution)/shard_map/all_gather | solution.py:42
  81.3 43.5 %copy-start.16 = (f32[128]{0:T(128)}, f32[128]{0:T(128)S(1)}, u32[]{:S(2)}) copy-start(f32[128]{0:T(128)S(1)} %add_rsqrt_fusion.2) | copy-start | bytes 1540
  126.8 4.7 copy-start.7
  127.1 4.4 copy-start.10
  127.7 16.2 %copy-start.14 = (f32[128]{0:T(128)}, f32[128]{0:T(128)S(1)}, u32[]{:S(2)}) copy-start(f32[128]{0:T(128)S(1)} %get-tuple-element.17) | copy-start | bytes 1540
  131.5 114.1 %all-to-all-start.2 = ((f32[32,48,256]{2,1,0:T(8,128)}), f32[32,48,256]{2,1,0:T(8,128)S(1)}, u32[]{:S(2)}, u32[]{:S(2)}) async-start(f32[32,48,256]{2,1,0:T(8,128)} %bitcast.65), calls=%async_computation.3 | async-start | bytes 3145728 | tf_op jit(solution)/shard_map/all_to_all | solution.py:87
  143.8 99.3 %reduce-scatter.2.cloned.1.call-start = ((), (), s32[]{:S(2)}) async-start(), calls=%async_computation.5 | async-start | bytes 2228224 | tf_op jit(solution)/shard_map/reduce_scatter | solution.py:82
  147.8 581.3 %all-reduce.3.cloned.1.call-start = ((), (), s32[]{:S(2)}) async-start(), calls=%async_computation.6 | async-start | bytes 4194304 | tf_op jit(solution)/shard_map/psum | solution.py:106
  165.7 2.2 copy-start.8
  165.7 2.2 copy-start.11
  165.7 2.2 copy-start.15
  165.7 2.2 copy-start.17
  165.7 2.5 copy-start.4
  167.9 76.3 %copy-start.6 = (bf16[128,1024]{1,0:T(8,128)(2,1)S(1)}, bf16[128,1024]{1,0:T(8,128)(2,1)}, u32[]{:S(2)}) copy-start(bf16[128,1024]{1,0:T(8,128)(2,1)} %param.9) | copy-start | bytes 786436
  245.5 1.9 copy-start.12
  247.4 2.1 copy-start.18
  729.1 2.6 copy-start.2
Sparse Core Ops, SparseCore 0:
  58.7 63.1 all-gather.2
  149.4 93.6 reduce-scatter.1
  251.7 477.3 all-reduce.2
where the time goes:
time: 740 us
  waiting for transfers between devices  602 us (81%)
  local copies, waits for them, and re-layouts  36.8 us (5%)
  starting transfers between devices  33.7 us (5%)
  blocking collectives  25.8 us (3%)
  between operations  14.1 us (2%)
  matrix products  14 us (2%)
  other arithmetic  13.2 us (2%)
    psum x1, waiting for transfers between devices, local(): grad_user, grad_item = lax.psum((grad_user, grad_item), ('group', 'dev'))  477 us
    reduce_scatter x1, waiting for transfers between devices, local(): lax.psum_scatter(contract(cycle_grad, user_low, 0, 0), 'group', scatter_d...  73.5 us
    all_gather x1, waiting for transfers between devices, local(): lax.all_gather(item_low, 'group', axis=0, tiled=True)  40.5 us
    all_gather x1, blocking collectives, local(): lax.all_gather(item_ids, 'group', axis=0, tiled=True)  25.8 us
    all_to_all x1, starting transfers between devices, local(): lax.all_to_all(wanted.reshape(owner_count, capacity), 'dev', split_axis=0...  17 us
  transfers between devices with their start and end apart: 6, of which 4 were waited for; matrix products, arithmetic and copies ran while one was open for 5% of the time, Pallas kernels for 0%

commit v1 on v0

--- a/solution.py
+++ b/solution.py
@@ -1,11 +1,203 @@
 import jax
 import jax.numpy as jnp
 from jax import lax
+from jax.experimental import pallas as pl
+from jax.experimental.pallas import tpu as pltpu
 from jax.sharding import PartitionSpec as P
 
 sharpen = 20.0
 epsilon = 1e-06
-
+MESH = pl.DeviceIdType.MESH
+NX, NY, NZ = 4, 4, 16
+
+
+def place():
+    group, dev = lax.axis_index("group"), lax.axis_index("dev")
+    core, x, y_hi = group % 2, (group // 2) % NX, group // (2 * NX)
+    z, y_lo = dev // 2, dev % 2
+    return core, x, y_hi * 2 + y_lo, z
+
+
+def device_at(core, x, y, z):
+    return (((y // 2) * NX + x) * 2 + core, z * 2 + y % 2)
+
+
+def greet(partners):
+    barrier = pltpu.get_barrier_semaphore()
+    for partner in partners:
+        pl.semaphore_signal(barrier, inc=1, device_id=partner, device_id_type=MESH)
+    pl.semaphore_wait(barrier, len(partners))
+
+
+def remote(src, dst, send_sem, recv_sem, device):
+    return pltpu.make_async_remote_copy(
+        src_ref=src, dst_ref=dst, send_sem=send_sem, recv_sem=recv_sem, device_id=device, device_id_type=MESH
+    )
+
+
+HALF = 1024
+FOLD = 512
+PART = 128
+BIT = 32
+
+
+def reduce_all_kernel(
+    user_ref, item_ref, out_ref, mine, from_core, from_first, from_second, from_z, load_sem,
+    core_send, core_recv, first_send, first_recv, second_send, second_recv, z_send, z_recv,
+    zg_send, zg_recv, sg_send, sg_recv, fg_send, fg_recv, cg_send, cg_recv,
+):
+    core, x, y, z = place()
+    other = 1 - core
+    sibling = device_at(other, x, y, z)
+    loads = [
+        pltpu.make_async_copy(user_ref, mine.at[0], load_sem.at[0]),
+        pltpu.make_async_copy(item_ref, mine.at[1], load_sem.at[1]),
+    ]
+    for load in loads:
+        load.start()
+    along = [
+        [device_at(core, (x + k) % NX, y, z) for k in range(1, NX)],
+        [device_at(core, x, (y + k) % NY, z) for k in range(1, NY)],
+    ]
+    along_z = [device_at(core, x, y, (z + k) % NZ) for k in range(1, NZ)]
+    greet([sibling] + along[0] + along[1] + along_z)
+    for load in loads:
+        load.wait()
+    first_at, second_at = [x, y], [y, x]
+
+    def part_rows(fold, part):
+        return pl.ds(pl.multiple_of(fold * FOLD + part * PART, PART), PART)
+
+    def bit_rows(fold, part, bit):
+        return pl.ds(pl.multiple_of(fold * FOLD + part * PART + bit * BIT, BIT), BIT)
+
+    def tile_of(at):
+        fold = at // 8
+        part = x + fold * (y - x)
+        bit = y + fold * (x - y)
+        row = fold * FOLD + part * PART + bit * BIT + ((at // 2) % 4) * 8
+        return pl.ds(pl.multiple_of(row, 8), 8), pl.ds(pl.multiple_of((at % 2) * 128, 128), 128)
+
+    order = [(k, fold) for k in (1, 2, 3, 0) for fold in (0, 1)]
+    core_copies = []
+    for n, (k, fold) in enumerate(order):
+        rows = part_rows(fold, (first_at[fold] + k) % 4)
+        copy = remote(mine.at[other, rows], from_core.at[n], core_send.at[n], core_recv.at[n], sibling)
+        copy.start()
+        core_copies.append(copy)
+    first_copies = []
+    for n, (k, fold) in enumerate(order):
+        rows = part_rows(fold, (first_at[fold] + k) % 4)
+        core_copies[n].wait_recv()
+        mine[core, rows] += from_core[n]
+        if k:
+            copy = remote(
+                mine.at[core, rows], from_first.at[fold, k - 1], first_send.at[fold, k - 1],
+                first_recv.at[fold, k - 1], along[fold][k - 1],
+            )
+            copy.start()
+            first_copies.append((copy, k, fold))
+    for copy, k, fold in first_copies:
+        copy.wait_recv()
+    second_copies = []
+    for k in (1, 2, 3, 0):
+        for fold in (0, 1):
+            at = (second_at[fold] + k) % 4
+            rows = bit_rows(fold, first_at[fold], at)
+            near = pl.ds(pl.multiple_of(at * BIT, BIT), BIT)
+            mine[core, rows] += from_first[fold, 0, near] + from_first[fold, 1, near] + from_first[fold, 2, near]
+            if k:
+                copy = remote(
+                    mine.at[core, rows], from_second.at[fold, k - 1], second_send.at[fold, k - 1],
+                    second_recv.at[fold, k - 1], along[1 - fold][k - 1],
+                )
+                copy.start()
+                second_copies.append((copy, k, fold))
+    for copy, k, fold in second_copies:
+        copy.wait_recv()
+    for fold in (0, 1):
+        rows = bit_rows(fold, first_at[fold], second_at[fold])
+        mine[core, rows] += from_second[fold, 0] + from_second[fold, 1] + from_second[fold, 2]
+    z_copies = []
+    for k in range(1, NZ):
+        rows, columns = tile_of((z + k) % NZ)
+        copy = remote(
+            mine.at[core, rows, columns], from_z.at[k - 1], z_send.at[k - 1], z_recv.at[k - 1], along_z[k - 1]
+        )
+        copy.start()
+        z_copies.append(copy)
+    rows, columns = tile_of(z)
+    total = mine[core, rows, columns]
+    for k, copy in enumerate(z_copies):
+        copy.wait_recv()
+        total = total + from_z[k]
+    out_ref[core, rows, columns] = total
+    gathers = []
+    for k in range(1, NZ):
+        tile = out_ref.at[core, rows, columns]
+        copy = remote(tile, tile, zg_send.at[k - 1], zg_recv.at[k - 1], along_z[k - 1])
+        copy.start()
+        gathers.append(copy)
+    for k in range(1, NZ):
+        tile_rows, tile_columns = tile_of((z + NZ - k) % NZ)
+        tile = out_ref.at[core, tile_rows, tile_columns]
+        remote(tile, tile, zg_send.at[k - 1], zg_recv.at[k - 1], along_z[k - 1]).wait_recv()
+    for k in (1, 2, 3):
+        for fold in (0, 1):
+            bit = out_ref.at[core, bit_rows(fold, first_at[fold], second_at[fold])]
+            copy = remote(bit, bit, sg_send.at[fold, k - 1], sg_recv.at[fold, k - 1], along[1 - fold][k - 1])
+            copy.start()
+            gathers.append(copy)
+    for k in (1, 2, 3):
+        for fold in (0, 1):
+            bit = out_ref.at[core, bit_rows(fold, first_at[fold], (second_at[fold] + 4 - k) % 4)]
+            remote(bit, bit, sg_send.at[fold, k - 1], sg_recv.at[fold, k - 1], along[1 - fold][k - 1]).wait_recv()
+    for k in (1, 2, 3):
+        for fold in (0, 1):
+            part = out_ref.at[core, part_rows(fold, first_at[fold])]
+            copy = remote(part, part, fg_send.at[fold, k - 1], fg_recv.at[fold, k - 1], along[fold][k - 1])
+            copy.start()
+            gathers.append(copy)
+    for k in (0, 1, 2, 3):
+        for fold in (0, 1):
+            rows = part_rows(fold, (first_at[fold] + 4 - k) % 4)
+            part = out_ref.at[core, rows]
+            if k:
+                remote(part, part, fg_send.at[fold, k - 1], fg_recv.at[fold, k - 1], along[fold][k - 1]).wait_recv()
+            copy = remote(part, part, cg_send.at[fold, k], cg_recv.at[fold, k], sibling)
+            copy.start()
+            gathers.append(copy)
+    for k in (0, 1, 2, 3):
+        for fold in (0, 1):
+            part = out_ref.at[other, part_rows(fold, (first_at[fold] + 4 - k) % 4)]
+            remote(part, part, cg_send.at[fold, k], cg_recv.at[fold, k], sibling).wait_recv()
+    for copy in core_copies + [c for c, _, _ in first_copies + second_copies] + z_copies + gathers:
+        copy.wait_send()
+
+
+def reduce_all(grad_user, grad_item):
+    dma = pltpu.SemaphoreType.DMA
+    out = pl.pallas_call(
+        reduce_all_kernel,
+        out_shape=jax.ShapeDtypeStruct((2, HALF, 256), jnp.float32),
+        in_specs=[pl.BlockSpec(memory_space=pl.ANY)] * 2,
+        out_specs=pl.BlockSpec(memory_space=pltpu.VMEM),
+        scratch_shapes=[
+            pltpu.VMEM((2, HALF, 256), jnp.float32),
+            pltpu.VMEM((8, PART, 256), jnp.float32),
+            pltpu.VMEM((2, 3, PART, 256), jnp.float32),
+            pltpu.VMEM((2, 3, BIT, 256), jnp.float32),
+            pltpu.VMEM((NZ - 1, 8, 128), jnp.float32),
+            dma((2,)),
+            dma((8,)), dma((8,)), dma((2, 3)), dma((2, 3)), dma((2, 3)), dma((2, 3)), dma((NZ - 1,)), dma((NZ - 1,)),
+            dma((NZ - 1,)), dma((NZ - 1,)), dma((2, 3)), dma((2, 3)), dma((2, 3)), dma((2, 3)), dma((2, 4)), dma((2, 4)),
+        ],
+        compiler_params=pltpu.CompilerParams(
+            collective_id=0, has_side_effects=True, vmem_limit_bytes=24 * 1024 * 1024
+        ),
+        name="reduce_all",
+    )(grad_user, grad_item)
+    return out[0], out[1]
 
 def project(features, weight):
     hidden = jnp.dot(features, weight, preferred_element_type=jnp.float32)
@@ -103,7 +295,7 @@
     item_back = unnormalize(item_unit, item_inv, item_up)
     grad_user = contract(user_feat, user_back, 0, 0)
     grad_item = contract(item_feat, item_back, 0, 0) + corpus_grad
-    grad_user, grad_item = lax.psum((grad_user, grad_item), ("group", "dev"))
+    grad_user, grad_item = reduce_all(grad_user, grad_item)
     return (loss, grad_user, grad_item)
 
 

time: 740 us -> 321 us (0.43)
  waiting for transfers between devices: 602 us -> 129 us
  Pallas kernels: 0 us -> 59.7 us
    psum x1 -> x0, waiting for transfers between devices: 477 us -> none  [local(): grad_user, grad_item = lax.psum((grad_user, grad_item), ('group', 'dev'))]
    pallas_call x0 -> x1, Pallas kernels: none -> 59.7 us  [reduce_all(): pl.pallas_call(reduce_all_kernel, out_shape=jax.ShapeDtypeStruct((2, HALF...]
  transfers between devices with their start and end apart: 6 -> 5, of which waited for: 4 -> 3; matrix products, arithmetic and copies ran while one was open for 5% -> 9% of each run, Pallas kernels for 0% -> 0%
where the time goes in v1:
time: 321 us; the launch traced here: 320 us
  waiting for transfers between devices  129 us (40%)
  Pallas kernels  59.7 us (19%)
  starting transfers between devices  33.7 us (10%)
  local copies, waits for them, and re-layouts  31.6 us (10%)
  blocking collectives  25.8 us (8%)
  between operations  14.4 us (4%)
  matrix products  13.2 us (4%)
  other arithmetic  12.6 us (4%)
    reduce_scatter x1, waiting for transfers between devices, local(): lax.psum_scatter(contract(cycle_grad, user_low, 0, 0), 'group', scatter_d...  78.6 us
    pallas_call x1, Pallas kernels, reduce_all(): pl.pallas_call(reduce_all_kernel, out_shape=jax.ShapeDtypeStruct((2, HALF...  59.7 us
    all_gather x1, waiting for transfers between devices, local(): lax.all_gather(item_low, 'group', axis=0, tiled=True)  40.5 us
    all_gather x1, blocking collectives, local(): lax.all_gather(item_ids, 'group', axis=0, tiled=True)  25.8 us
    all_to_all x1, starting transfers between devices, local(): lax.all_to_all(wanted.reshape(owner_count, capacity), 'dev', split_axis=0...  17 us
    all_to_all x1, starting transfers between devices, local(): lax.all_to_all(placed.reshape(owner_count, capacity, width), 'dev', split...  12.3 us
    all_to_all x1, waiting for transfers between devices, local(): lax.all_to_all(wanted.reshape(owner_count, capacity), 'dev', split_axis=0...  10.4 us
    gather x1, local copies, waits for them, and re-layouts, local(): corpus_inv[safe_rows]  9.43 us
  transfers between devices with their start and end apart: 5, of which 3 were waited for; matrix products, arithmetic and copies ran while one was open for 9% of the time, Pallas kernels for 0%

profile of v1, /device:TPU:1, one launch (start us, length us, event | category | flops | bytes accessed | tf_op | source)
XLA Modules:
  0.0 320.4 jit_solution(6752418104844577758)
XLA Ops:
  7.2 0.7 fusion.22
  7.9 1.2 reduce-window.6
  9.3 0.8 fusion.17
  10.1 0.7 compare_select_fusion.2
  10.8 2.6 scatter_custom_fusion
  13.4 0.7 all_to_all.12
  14.1 17.0 %all-to-all-start = ((s32[32,1,48]{2,1,0:T(1,128)}), s32[32,1,48]{2,1,0:T(1,128)S(1)}, u32[]{:S(2)}, u32[]{:S(2)}) async-start(s32[32,1,48]{2,1,0:T(1,128)} %all_to_all.12), calls=%async_computation | async-start | bytes 32768 | tf_op jit(solution)/shard_map/all_to_all | solution.py:244
  31.2 1.4 multiply_reduce_fusion.1
  32.8 10.4 %all-to-all-done = s32[32,1,48]{2,1,0:T(1,128)S(1)} async-done(((s32[32,1,48]{2,1,0:T(1,128)}), s32[32,1,48]{2,1,0:T(1,128)S(1)}, u32[]{:S(2)}, u32[]{:S(2)}) %all-to-all-start) | async-done | bytes 6176 | tf_op jit(solution)/shard_map/all_to_all | solution.py:244
  44.5 5.4 %gather_fusion = bf16[1536,256]{1,0:T(8,128)(2,1)} fusion(bf16[256,256]{1,0:T(8,128)(2,1)S(1)} %copy.23, s32[2048]{0:T(1024)S(1)} %pad_clamp_fusion), kind=kCustom, calls=%fused_computation | custom fusion | bytes 1579008 | tf_op jit(solution)/shard_map/gather | solution.py:250
  49.9 4.1 %all-to-all-start.1 = ((bf16[32,48,256]{2,1,0:T(8,128)(2,1)}), bf16[32,48,256]{2,1,0:T(8,128)(2,1)S(1)}, u32[]{:S(2)}, u32[]{:S(2)}) async-start(bf16[32,48,256]{2,1,0:T(8,128)(2,1)} %bitcast.7), calls=%async_computation.1 | async-start | bytes 1572864 | tf_op jit(solution)/shard_map/all_to_all | solution.py:251
  54.4 0.7 multiply_convert_fusion.4
  55.1 25.8 %all-gather = s32[16,1,128]{2,1,0:T(1,128)S(1)} all-gather(s32[1,1,128]{2,1,0:T(1,128)S(1)} %bitcast.79), channel_id=1, replica_groups=mesh['group'=16,'dev'=32] {'group'}, dimensions={0}, use_global_device_ids=true | all-gather | bytes 8704 | tf_op jit(solution)/shard_map/all_gather | solution.py:235
  81.4 40.5 %all-gather.3.cloned.1.call-done = bf16[2048,256]{1,0:T(8,128)(2,1)} async-done(((bf16[128,256]{1,0:T(8,128)(2,1)}), bf16[2048,256]{1,0:T(8,128)(2,1)}) %all-gather.3.cloned.1.call-update) | async-done | bytes 1048592 | tf_op jit(solution)/shard_map/all_gather | solution.py:234
  121.9 2.9 fusion.13
  124.8 1.9 gather_fusion.1
  128.0 3.5 %scatter_custom_fusion.1 = f32[1536,256]{1,0:T(8,128)} fusion(s32[512]{0:T(512)S(1)} %bitcast.77, f32[512,256]{1,0:T(8,128)S(1)} %fusion.26, f32[]{:T(128)} %constant.15.clone.1), kind=kCustom, calls=%fused_computation.28 | custom fusion | bytes 1572868 | tf_op jit(solution)/shard_map/scatter | solution.py:278
  131.4 12.3 %all-to-all-start.2 = ((f32[32,48,256]{2,1,0:T(8,128)}), f32[32,48,256]{2,1,0:T(8,128)S(1)}, u32[]{:S(2)}, u32[]{:S(2)}) async-start(f32[32,48,256]{2,1,0:T(8,128)} %bitcast.69), calls=%async_computation.3 | async-start | bytes 3145728 | tf_op jit(solution)/shard_map/all_to_all | solution.py:279
  144.0 2.1 multiply_convert_fusion
  146.1 1.8 fusion.30
  148.1 9.4 %gather_fusion.3 = f32[1536]{0:T(1024)S(1)} fusion(f32[256]{0:T(256)S(1)} %add_rsqrt_fusion, s32[2048]{0:T(1024)S(1)} %pad_clamp_fusion), kind=kCustom, calls=%fused_computation.3 | custom fusion | bytes 18432 | tf_op jit(solution)/shard_map/gather | solution.py:282
  157.6 4.6 %gather_fusion.2 = f32[1536,256]{1,0:T(8,128)} fusion(f32[256,256]{1,0:T(8,128)S(1)} %copy.25, s32[2048]{0:T(1024)S(1)} %pad_clamp_fusion), kind=kCustom, calls=%fused_computation.2 | custom fusion | bytes 3151872 | tf_op jit(solution)/shard_map/gather | solution.py:282
  162.2 1.6 fusion.29
  164.6 78.6 %reduce-scatter.2.cloned.1.call-done = f32[128,256]{1,0:T(8,128)} async-done(((f32[2048,256]{1,0:T(8,128)}), f32[128,256]{1,0:T(8,128)}) %reduce-scatter.2.cloned.1.call-update) | async-done | bytes 131088 | tf_op jit(solution)/shard_map/reduce_scatter | solution.py:274
  243.1 1.1 multiply_reduce_fusion.2
  244.2 2.4 fusion.14
  246.6 1.8 multiply_reduce_fusion
  248.5 2.1 fusion.1
  251.0 0.8 copy-done.1
  251.8 0.7 fusion.5.item_ref
  252.5 59.7 %reduce_all.1 = f32[2,1024,256]{2,1,0:T(8,128)S(1)} custom-call(f32[1024,256]{1,0:T(8,128)S(1)} %convolution_bitcast_fusion.user_ref, f32[1024,256]{1,0:T(8,128)S(1)} %fusion.5.item_ref), custom_call_target="tpu_custom_call" | custom-call | tf_op jit(solution)/shard_map/reduce_all/pallas_call | solution.py:180
  312.1 1.5 slice_bitcast_fusion
  (57 shorter events, 5.4 us)
Async XLA Ops:
  7.2 24.0 %copy-start = (bf16[256,1024]{1,0:T(8,128)(2,1)S(1)}, bf16[256,1024]{1,0:T(8,128)(2,1)}, u32[]{:S(2)}) copy-start(bf16[256,1024]{1,0:T(8,128)(2,1)} %param.11) | copy-start | bytes 1572868
  14.1 29.0 %all-to-all-start = ((s32[32,1,48]{2,1,0:T(1,128)}), s32[32,1,48]{2,1,0:T(1,128)S(1)}, u32[]{:S(2)}, u32[]{:S(2)}) async-start(s32[32,1,48]{2,1,0:T(1,128)} %all_to_all.12), calls=%async_computation | async-start | bytes 32768 | tf_op jit(solution)/shard_map/all_to_all | solution.py:244
  49.9 4.1 %copy-start.2 = (bf16[1024,256]{1,0:T(8,128)(2,1)S(1)}, bf16[1024,256]{1,0:T(8,128)(2,1)}, u32[]{:S(2)}) copy-start(bf16[1024,256]{1,0:T(8,128)(2,1)} %param.15) | copy-start | bytes 1572868
  49.9 4.1 %copy-start.5 = (bf16[128,1024]{1,0:T(8,128)(2,1)S(1)}, bf16[128,1024]{1,0:T(8,128)(2,1)}, u32[]{:S(2)}) copy-start(bf16[128,1024]{1,0:T(8,128)(2,1)} %param.9) | copy-start | bytes 786436
  49.9 5.2 %copy-start.11 = (s32[128]{0:T(128)S(1)}, s32[128]{0:T(128)}, u32[]{:S(2)}) copy-start(s32[128]{0:T(128)} %param.10) | copy-start | bytes 1540
  49.9 31.1 %copy-start.3 = (bf16[128,1024]{1,0:T(8,128)(2,1)S(1)}, bf16[128,1024]{1,0:T(8,128)(2,1)}, u32[]{:S(2)}) copy-start(bf16[128,1024]{1,0:T(8,128)(2,1)} %param.8) | copy-start | bytes 786436
  49.9 31.1 %copy-start.8 = (bf16[1024,256]{1,0:T(8,128)(2,1)S(1)}, bf16[1024,256]{1,0:T(8,128)(2,1)}, u32[]{:S(2)}) copy-start(bf16[1024,256]{1,0:T(8,128)(2,1)} %param.14) | copy-start | bytes 1572868
  49.9 74.9 %all-to-all-start.1 = ((bf16[32,48,256]{2,1,0:T(8,128)(2,1)}), bf16[32,48,256]{2,1,0:T(8,128)(2,1)S(1)}, u32[]{:S(2)}, u32[]{:S(2)}) async-start(bf16[32,48,256]{2,1,0:T(8,128)(2,1)} %bitcast.7), calls=%async_computation.1 | async-start | bytes 1572864 | tf_op jit(solution)/shard_map/all_to_all | solution.py:251
  54.0 67.9 %all-gather.3.cloned.1.call-start = ((), (), s32[]{:S(2)}) async-start(), calls=%async_computation.4 | async-start | bytes 1114112 | tf_op jit(solution)/shard_map/all_gather | solution.py:234
  126.8 4.7 %copy-start.6 = (bf16[512,256]{1,0:T(8,128)(2,1)}, bf16[512,256]{1,0:T(8,128)(2,1)S(1)}, u32[]{:S(2)}) copy-start(bf16[512,256]{1,0:T(8,128)(2,1)S(1)} %gather_fusion.1) | copy-start | bytes 786436
  127.1 4.4 %copy-start.9 = (f32[128,512]{1,0:T(8,128)}, f32[128,512]{1,0:T(8,128)S(1)}, u32[]{:S(2)}) copy-start(f32[128,512]{1,0:T(8,128)S(1)} %get-tuple-element.19) | copy-start | bytes 786436
  131.4 115.2 %all-to-all-start.2 = ((f32[32,48,256]{2,1,0:T(8,128)}), f32[32,48,256]{2,1,0:T(8,128)S(1)}, u32[]{:S(2)}, u32[]{:S(2)}) async-start(f32[32,48,256]{2,1,0:T(8,128)} %bitcast.69), calls=%async_computation.3 | async-start | bytes 3145728 | tf_op jit(solution)/shard_map/all_to_all | solution.py:279
  143.8 99.4 %reduce-scatter.2.cloned.1.call-start = ((), (), s32[]{:S(2)}) async-start(), calls=%async_computation.5 | async-start | bytes 2228224 | tf_op jit(solution)/shard_map/reduce_scatter | solution.py:274
  162.2 1.6 copy-start.7
  162.2 1.6 copy-start.10
  162.2 2.0 copy-start.4
  250.5 1.2 copy-start.1
Sparse Core Ops, SparseCore 0:
  58.7 63.1 all-gather.2
  149.4 93.6 reduce-scatter.1

commit v2 on v1

--- a/solution.py
+++ b/solution.py
@@ -199,104 +199,329 @@
     )(grad_user, grad_item)
     return out[0], out[1]
 
+TOK, OWN, NEG, WIDE, E = 128, 256, 512, 1024, 256
+NG, ND = 16, 32
+f32, bf16 = jnp.float32, jnp.bfloat16
+
+
+def dot(left, right, left_dim=1, right_dim=0):
+    return lax.dot_general(left, right, (((left_dim,), (right_dim,)), ((), ())), preferred_element_type=f32)
+
+
 def project(features, weight):
-    hidden = jnp.dot(features, weight, preferred_element_type=jnp.float32)
+    hidden = dot(features, weight)
     inverse = lax.rsqrt(jnp.sum(hidden * hidden, axis=-1, keepdims=True) + epsilon)
-    return (hidden * inverse, inverse)
+    return hidden * inverse, inverse
 
 
 def unnormalize(unit, inverse, upstream):
     along = jnp.sum(unit * upstream, axis=-1, keepdims=True)
-    return ((upstream - unit * along) * inverse).astype(jnp.bfloat16)
-
-
-def contract(left, right, left_dim, right_dim):
-    return lax.dot_general(
-        left, right, (((left_dim,), (right_dim,)), ((), ())), preferred_element_type=jnp.float32
+    return ((upstream - unit * along) * inverse).astype(bf16)
+
+
+def local_grads_kernel(
+    user_feat, item_feat, corpus_feat, user_weight, item_weight, ids_in, codes_in,
+    loss_ref, grad_user_ref, grad_item_ref,
+    uf, itf, cf, uw, iw, corp, gus, cyc, ids, codes, pair_codes, tot_g, tot_d,
+    select, sel_out, sel_in, cexp, unit_u, unit_i, unit_c, inv_u, inv_i, inv_c, owned,
+    load_sem, ids_send, ids_recv, codes_send, codes_recv, pair_send, pair_recv, tg_send, tg_recv, td_send, td_recv,
+    zc_send, zc_recv, zu_send, zu_recv, yu_send, yu_recv, ys_send, ys_recv,
+    yh_send, yh_recv, x_send, x_recv, c_send, c_recv,
+):
+    core, x, y, z = place()
+    y_hi, y_lo = y // 2, y % 2
+    group, dev = lax.axis_index("group"), lax.axis_index("dev")
+    factor = sharpen / TOK
+    loads = [
+        pltpu.make_async_copy(src, dst, load_sem.at[n])
+        for n, (src, dst) in enumerate([
+            (corpus_feat, cf), (item_weight, iw), (user_feat, uf), (user_weight, uw), (item_feat, itf),
+            (ids_in, ids.at[group]), (codes_in, codes.at[dev]),
+        ])
+    ]
+    for load in loads:
+        load.start()
+    group_peers = [(lax.rem(group + k, NG), dev) for k in range(1, NG)]
+    dev_peers = [(group, lax.rem(dev + k, ND)) for k in range(1, ND)]
+    sibling = device_at(1 - core, x, y, z)
+    y_partner = device_at(core, x, y_hi * 2 + 1 - y_lo, z)
+    y_far = device_at(core, x, (1 - y_hi) * 2 + y_lo, z)
+    x_peers = [device_at(core, (x + k) % NX, y, z) for k in range(1, NX)]
+    z_peers = [device_at(core, x, y, (z + 1) % NZ), device_at(core, x, y, (z + NZ - 1) % NZ)]
+    sends = []
+
+    def send(src, dst, send_sem, recv_sem, device):
+        copy = remote(src, dst, send_sem, recv_sem, device)
+        copy.start()
+        sends.append(copy)
+
+    def arrived(dst, send_sem, recv_sem, device):
+        remote(dst, dst, send_sem, recv_sem, device).wait_recv()
+
+    barrier = pltpu.get_barrier_semaphore()
+    for partner in group_peers + dev_peers:
+        pl.semaphore_signal(barrier, inc=1, device_id=partner, device_id_type=MESH)
+
+    loads[0].wait()
+    loads[1].wait()
+    unit, inverse = project(cf[...], iw[...])
+    unit_c[...] = unit
+    inv_c[...] = inverse
+    corp[z] = unit.astype(bf16).reshape(2, TOK, E)
+    pl.semaphore_wait(barrier, NG - 1 + ND - 1)
+
+    def z_send(buf, at, s, e, way, send_sem, recv_sem):
+        send(buf.at[at, e], buf.at[at, e], send_sem.at[way, s - 1, e], recv_sem.at[way, s - 1, e], z_peers[way])
+
+    def source(way, s):
+        return (z + NZ - s) % NZ if way == 0 else (z + s) % NZ
+
+    def z_step(buf, s, send_sem, recv_sem):
+        for e in (0, 1):
+            for way in (0, 1):
+                if s == 8 and e != way:
+                    continue
+                at = source(way, s)
+                arrived(buf.at[at, e], send_sem.at[way, s - 1, e], recv_sem.at[way, s - 1, e], z_peers[way])
+                if s < 7 or (s == 7 and e == way):
+                    z_send(buf, at, s + 1, e, way, send_sem, recv_sem)
+
+    for e in (0, 1):
+        for way in (0, 1):
+            z_send(corp, z, 1, e, way, zc_send, zc_recv)
+    loads[6].wait()
+    send(codes.at[dev], pair_codes, pair_send, pair_recv, y_partner)
+    for k in range(1, ND):
+        send(codes.at[dev], codes.at[dev], codes_send.at[k - 1], codes_recv.at[k - 1], dev_peers[k - 1])
+
+    loads[2].wait()
+    loads[3].wait()
+    unit, inverse = project(uf[...], uw[...])
+    unit_u[...] = unit
+    inv_u[...] = inverse
+    user_low = unit.astype(bf16)
+    cyc[group, 0] = user_low
+    gus[z, y_lo] = user_low
+    send(gus.at[z, y_lo], gus.at[z, y_lo], yu_send, yu_recv, y_partner)
+    loads[4].wait()
+    unit, inverse = project(itf[...], iw[...])
+    unit_i[...] = unit
+    inv_i[...] = inverse
+    item_low = unit.astype(bf16)
+    cyc[group, 1] = item_low
+    far_group = lax.rem(group + NG // 2, NG)
+    send(cyc.at[group], cyc.at[group], yh_send, yh_recv, y_far)
+    for k in range(1, NX):
+        send(cyc.at[group], cyc.at[group], x_send.at[0, k - 1], x_recv.at[0, k - 1], x_peers[k - 1])
+    send(cyc.at[group], cyc.at[group], c_send.at[0, 0], c_recv.at[0, 0], sibling)
+    loads[5].wait()
+    for k in range(1, NG):
+        send(ids.at[group], ids.at[group], ids_send.at[k - 1], ids_recv.at[k - 1], group_peers[k - 1])
+
+
+    def group_of(far, k, other):
+        row = y_hi + far * (1 - 2 * y_hi)
+        return (row * NX + (x + NX - k) % NX) * 2 + core + other * (1 - 2 * core)
+
+    arrived(pair_codes, pair_send, pair_recv, y_partner)
+    own_codes, their_codes = codes[dev], pair_codes[...]
+    code_row = jnp.concatenate(
+        [own_codes[n : n + 1] for n in range(4)] + [their_codes[n : n + 1] for n in range(4)], axis=1
     )
+    wide_rows = lax.broadcasted_iota(jnp.int32, (OWN, 2 * NEG), 0)
+
+    def select_from(at):
+        hot = (code_row - (at * 2 + y_lo) * OWN == wide_rows).astype(f32).astype(bf16)
+        return dot(corp[at].reshape(OWN, E), hot, 0, 0)
+
+    select[...] = select_from(z)
+    for s in range(1, 9):
+        z_step(corp, s, zc_send, zc_recv)
+        if s == 1:
+            arrived(cyc.at[far_group], yh_send, yh_recv, y_far)
+            for k in range(1, NX):
+                send(cyc.at[far_group], cyc.at[far_group], x_send.at[1, k - 1], x_recv.at[1, k - 1], x_peers[k - 1])
+            send(cyc.at[far_group], cyc.at[far_group], c_send.at[1, 0], c_recv.at[1, 0], sibling)
+        if s in (3, 5):
+            far = (s - 3) // 2
+            for k in range(1, NX):
+                block = cyc.at[group_of(far, k, 0)]
+                arrived(block, x_send.at[far, k - 1], x_recv.at[far, k - 1], x_peers[k - 1])
+                send(block, block, c_send.at[far, k], c_recv.at[far, k], sibling)
+        if s == 7:
+            arrived(gus.at[z, 1 - y_lo], yu_send, yu_recv, y_partner)
+            for e in (0, 1):
+                for way in (0, 1):
+                    z_send(gus, z, 1, e, way, zu_send, zu_recv)
+        if s < 8:
+            select[...] += select_from(source(0, s)) + select_from(source(1, s))
+        else:
+            select[...] += select_from(source(0, s))
+    sel_out[...] = select[:, NEG:].astype(bf16)
+    send(sel_out, sel_in, ys_send, ys_recv, y_partner)
+
+    for far in (0, 1):
+        for k in range(NX):
+            arrived(cyc.at[group_of(far, k, 1)], c_send.at[far, k], c_recv.at[far, k], sibling)
+    for k in range(1, NG):
+        arrived(ids.at[lax.rem(group + NG - k, NG)], ids_send.at[k - 1], ids_recv.at[k - 1], group_peers[k - 1])
+
+    tile_rows = lax.broadcasted_iota(jnp.int32, (TOK, TOK), 0)
+    tile_columns = lax.broadcasted_iota(jnp.int32, (TOK, TOK), 1)
+    eye = tile_rows == tile_columns
+
+    def to_row(column):
+        return jnp.sum(jnp.where(eye, column, 0.0), axis=0, keepdims=True)
+
+    own_ids = ids[group, 0:1].astype(f32)
+    ids_column = jnp.sum(jnp.where(eye, own_ids, 0.0), axis=1, keepdims=True)
+    user_low = cyc[group, 0]
+    item_low = cyc[group, 1]
+
+    def masks(g):
+        diagonal = tile_columns + g * TOK == tile_rows + group * TOK
+        same = ids[g, 0:1].astype(f32) == ids_column
+        return diagonal, jnp.logical_and(same, jnp.logical_not(diagonal))
+
+    def cycle_forward(g, carry):
+        sums, own = carry
+        logit = sharpen * dot(user_low, cyc[g, 1], 1, 1)
+        diagonal, hidden = masks(g)
+        value = jnp.where(hidden, 0.0, jnp.exp(logit))
+        cexp[g] = value
+        return sums + value, own + jnp.where(diagonal, logit, 0.0)
+
+    zeros = jnp.zeros((TOK, TOK), f32)
+    sums, own = lax.fori_loop(0, NG, cycle_forward, (zeros, zeros), unroll=2)
+    cycle_total = jnp.sum(sums, axis=1, keepdims=True)
+    own_logit = jnp.sum(own, axis=1, keepdims=True)
+
+    z_step(gus, 1, zu_send, zu_recv)
+    arrived(sel_in, ys_send, ys_recv, y_partner)
+    sample_low = (select[:, :NEG] + sel_in[...].astype(f32)).astype(bf16)
+    sample_exp = jnp.exp(sharpen * dot(user_low, sample_low))
+    total = cycle_total + jnp.sum(sample_exp, axis=1, keepdims=True)
+    total_row = to_row(total)
+    tot_g[group] = jnp.broadcast_to(total_row, (8, TOK))
+    tot_d[dev] = jnp.broadcast_to(total_row, (8, TOK))
+    for k in range(1, ND):
+        send(tot_d.at[dev], tot_d.at[dev], td_send.at[k - 1], td_recv.at[k - 1], dev_peers[k - 1])
+    for k in range(1, NG):
+        send(tot_g.at[group], tot_g.at[group], tg_send.at[k - 1], tg_recv.at[k - 1], group_peers[k - 1])
+    loss_ref[...] = jnp.broadcast_to(to_row(jnp.log(total) - own_logit), (8, TOK))
+
+    z_step(gus, 2, zu_send, zu_recv)
+    inverse_total = 1.0 / total
+
+    def user_backward(g, up):
+        diagonal = tile_columns + g * TOK == tile_rows + group * TOK
+        grad = ((cexp[g] * inverse_total - diagonal.astype(f32)) * factor).astype(bf16)
+        return up + dot(grad, cyc[g, 1])
+
+    sample_grad = (sample_exp * inverse_total * factor).astype(bf16)
+    user_up = lax.fori_loop(0, NG, user_backward, dot(sample_grad, sample_low, 1, 1), unroll=2)
+    user_back = unnormalize(unit_u[...], inv_u[...], user_up)
+    grad_user_ref[...] = dot(uf[...], user_back, 0, 0)
+
+    z_step(gus, 3, zu_send, zu_recv)
+    for k in range(1, NG):
+        arrived(tot_g.at[lax.rem(group + NG - k, NG)], tg_send.at[k - 1], tg_recv.at[k - 1], group_peers[k - 1])
+
+    def item_backward(g, up):
+        users = cyc[g, 0]
+        diagonal, hidden = masks(g)
+        value = jnp.where(hidden, 0.0, jnp.exp(sharpen * dot(item_low, users, 1, 1)))
+        grad = ((value * (1.0 / tot_g[g, 0:1]) - diagonal.astype(f32)) * factor).astype(bf16)
+        return up + dot(grad, users)
+
+    item_up = lax.fori_loop(0, NG, item_backward, jnp.zeros((TOK, E), f32), unroll=2)
+    item_back = unnormalize(unit_i[...], inv_i[...], item_up)
+    z_step(gus, 4, zu_send, zu_recv)
+    for k in range(1, ND):
+        at = lax.rem(dev + ND - k, ND)
+        arrived(codes.at[at], codes_send.at[k - 1], codes_recv.at[k - 1], dev_peers[k - 1])
+        arrived(tot_d.at[at], td_send.at[k - 1], td_recv.at[k - 1], dev_peers[k - 1])
+    owned[...] = jnp.zeros((OWN, E), f32)
+    corpus_low = corp[z].reshape(OWN, E)
+    code_rows = lax.broadcasted_iota(jnp.int32, (OWN, NEG), 0)
+    ones = jnp.ones((NEG, 128), bf16)
+
+    def corpus_backward(at, e):
+        users = gus[at, e]
+        holder = at * 2 + e
+        value = jnp.exp(sharpen * dot(corpus_low, users, 1, 1))
+        grad = (value * (1.0 / tot_d[holder, 0:1]) * factor).astype(bf16)
+        back = unnormalize(unit_c[...], inv_c[...], dot(grad, users)).astype(f32)
+        named = codes[holder]
+        row = jnp.concatenate([named[n : n + 1] for n in range(4)], axis=1)
+        hot = (row - dev * OWN == code_rows).astype(f32).astype(bf16)
+        count = dot(hot, ones)
+        owned[...] += jnp.concatenate([count, count], axis=1) * back
+
+    def near_backward(i, carry):
+        corpus_backward((z + NZ - 4 + i // 2) % NZ, i % 2)
+        return carry
+
+    lax.fori_loop(0, 18, near_backward, 0)
+    for s in range(5, 9):
+        z_step(gus, s, zu_send, zu_recv)
+
+        def step_backward(i, carry, s=s):
+            corpus_backward((z + NZ - s + (i // 2) * 2 * s) % NZ, i % 2)
+            return carry
+
+        lax.fori_loop(0, 4 if s < 8 else 2, step_backward, 0)
+    high = owned[...].astype(bf16)
+    low = (owned[...] - high.astype(f32)).astype(bf16)
+    features = jnp.concatenate([itf[...], cf[...], cf[...]], axis=0)
+    backs = jnp.concatenate([item_back, high, low], axis=0)
+    grad_item_ref[...] = dot(features, backs, 0, 0)
+    for copy in sends:
+        copy.wait_send()
+
+
+def local_grads(user_feat, item_feat, corpus_feat, user_weight, item_weight, ids, codes):
+    dma, vmem = pltpu.SemaphoreType.DMA, pltpu.VMEM
+    pairs = lambda *shape: [dma(shape), dma(shape)]
+    return pl.pallas_call(
+        local_grads_kernel,
+        out_shape=[
+            jax.ShapeDtypeStruct((8, TOK), f32),
+            jax.ShapeDtypeStruct((WIDE, E), f32),
+            jax.ShapeDtypeStruct((WIDE, E), f32),
+        ],
+        in_specs=[pl.BlockSpec(memory_space=pl.ANY)] * 7,
+        out_specs=[pl.BlockSpec(memory_space=pltpu.VMEM)] * 3,
+        scratch_shapes=[
+            vmem((TOK, WIDE), bf16), vmem((TOK, WIDE), bf16), vmem((OWN, WIDE), bf16),
+            vmem((WIDE, E), bf16), vmem((WIDE, E), bf16),
+            vmem((NZ, 2, TOK, E), bf16), vmem((NZ, 2, TOK, E), bf16), vmem((NG, 2, TOK, E), bf16),
+            vmem((NG, 8, 128), jnp.int32), vmem((ND, 8, 128), jnp.int32), vmem((8, 128), jnp.int32),
+            vmem((NG, 8, 128), f32), vmem((ND, 8, 128), f32),
+            vmem((E, 2 * NEG), f32), vmem((E, NEG), bf16), vmem((E, NEG), bf16), vmem((NG, TOK, TOK), f32),
+            vmem((TOK, E), f32), vmem((TOK, E), f32), vmem((OWN, E), f32),
+            vmem((TOK, 1), f32), vmem((TOK, 1), f32), vmem((OWN, 1), f32), vmem((OWN, E), f32),
+            dma((7,)), *pairs(NG - 1), *pairs(ND - 1), *pairs(), *pairs(NG - 1), *pairs(ND - 1),
+            *pairs(2, 8, 2), *pairs(2, 8, 2), *pairs(), *pairs(), *pairs(), *pairs(2, 3), *pairs(2, 4),
+        ],
+        compiler_params=pltpu.CompilerParams(
+            collective_id=1, has_side_effects=True, vmem_limit_bytes=48 * 1024 * 1024
+        ),
+        name="local_grads",
+    )(user_feat, item_feat, corpus_feat, user_weight, item_weight, ids, codes)
 
 
 def local(
     user_feat, item_feat, item_ids, corpus_feat, neg_owner, neg_row, user_weight, item_weight
 ):
-    tok_rows = user_feat.shape[0]
-    owner_count = lax.axis_size("dev")
-    sample_count = neg_row.shape[0]
-    capacity = 3 * sample_count // owner_count
-    width = user_weight.shape[1]
-    owned_rows = corpus_feat.shape[0]
-    factor = sharpen / tok_rows
-    user_unit, user_inv = project(user_feat, user_weight)
-    user_low = user_unit.astype(jnp.bfloat16)
-    item_unit, item_inv = project(item_feat, item_weight)
-    item_low = item_unit.astype(jnp.bfloat16)
-    cycle_items, cycle_ids = (
-        lax.all_gather(item_low, "group", axis=0, tiled=True),
-        lax.all_gather(item_ids, "group", axis=0, tiled=True),
+    ids = jnp.broadcast_to(item_ids[None, :], (8, TOK))
+    code = neg_owner[:, 0] * OWN + neg_row
+    codes = jnp.concatenate([code.reshape(4, 128)] * 2, axis=0)
+    loss, grad_user, grad_item = local_grads(
+        user_feat, item_feat, corpus_feat, user_weight, item_weight, ids, codes
     )
-    owners = neg_owner[:, 0]
-    owner_hot = (owners[:, None] == jnp.arange(owner_count, dtype=jnp.int32)[None, :]).astype(
-        jnp.int32
-    )
-    earlier = jnp.cumsum(owner_hot, axis=0) - owner_hot
-    slot = owners * capacity + jnp.sum(earlier * owner_hot, axis=1)
-    wanted = jnp.full((owner_count * capacity,), -1, jnp.int32).at[slot].set(neg_row)
-    requests = lax.all_to_all(
-        wanted.reshape(owner_count, capacity), "dev", split_axis=0, concat_axis=0, tiled=True
-    ).reshape(-1)
-    valid = requests >= 0
-    safe_rows = jnp.where(valid, requests, 0)
-    corpus_unit, corpus_inv = project(corpus_feat, item_weight)
-    reply = corpus_unit.astype(jnp.bfloat16)[safe_rows].reshape(owner_count, capacity, width)
-    arrived = lax.all_to_all(reply, "dev", split_axis=0, concat_axis=0, tiled=True).reshape(
-        owner_count * capacity, width
-    )
-    sample_low = arrived[slot]
-    cycle_logit = sharpen * contract(user_low, cycle_items, 1, 1)
-    sample_logit = sharpen * contract(user_low, sample_low, 1, 1)
-    columns = jnp.arange(cycle_ids.shape[0], dtype=jnp.int32)
-    here = lax.axis_index("group")
-    own_column = here * tok_rows + jnp.arange(tok_rows, dtype=jnp.int32)
-    diagonal = columns[None, :] == own_column[:, None]
-    keep = jnp.logical_not((cycle_ids[None, :] == item_ids[:, None]) & jnp.logical_not(diagonal))
-    cycle_exp = jnp.where(keep, jnp.exp(cycle_logit), jnp.float32(0.0))
-    sample_exp = jnp.exp(sample_logit)
-    total = jnp.sum(cycle_exp, axis=1) + jnp.sum(sample_exp, axis=1)
-    own_logit = jnp.sum(jnp.where(diagonal, cycle_logit, jnp.float32(0.0)), axis=1)
-    loss = jnp.log(total) - own_logit
-    cycle_grad = ((cycle_exp / total[:, None] - diagonal.astype(jnp.float32)) * factor).astype(
-        jnp.bfloat16
-    )
-    sample_grad = (sample_exp / total[:, None] * factor).astype(jnp.bfloat16)
-    user_up = jnp.dot(cycle_grad, cycle_items, preferred_element_type=jnp.float32) + jnp.dot(
-        sample_grad, sample_low, preferred_element_type=jnp.float32
-    )
-    item_up = lax.psum_scatter(
-        contract(cycle_grad, user_low, 0, 0), "group", scatter_dimension=0, tiled=True
-    )
-    sample_up = contract(sample_grad, user_low, 0, 0)
-    placed = jnp.zeros((owner_count * capacity, width), jnp.float32).at[slot].set(sample_up)
-    returned = lax.all_to_all(
-        placed.reshape(owner_count, capacity, width), "dev", split_axis=0, concat_axis=0, tiled=True
-    ).reshape(owner_count * capacity, width)
-    slot_back = unnormalize(corpus_unit[safe_rows], corpus_inv[safe_rows], returned)
-    owner_table = (
-        (jnp.arange(owned_rows, dtype=jnp.int32)[:, None] == requests[None, :]) & valid[None, :]
-    ).astype(jnp.bfloat16)
-    owned_back = jnp.dot(owner_table, slot_back, preferred_element_type=jnp.float32)
-    corpus_grad = lax.dot_general(
-        corpus_feat.astype(jnp.float32),
-        owned_back,
-        (((0,), (0,)), ((), ())),
-        precision=lax.Precision.HIGHEST,
-        preferred_element_type=jnp.float32,
-    )
-    user_back = unnormalize(user_unit, user_inv, user_up)
-    item_back = unnormalize(item_unit, item_inv, item_up)
-    grad_user = contract(user_feat, user_back, 0, 0)
-    grad_item = contract(item_feat, item_back, 0, 0) + corpus_grad
     grad_user, grad_item = reduce_all(grad_user, grad_item)
-    return (loss, grad_user, grad_item)
+    return loss[0], grad_user, grad_item
 
 
 def solution(mesh):

time: 321 us -> 158 us (0.49)
  waiting for transfers between devices: 129 us -> 0 us
  Pallas kernels: 59.7 us -> 148 us
  starting transfers between devices: 33.7 us -> 0 us
  blocking collectives: 25.8 us -> 0 us
  local copies, waits for them, and re-layouts: 31.6 us -> 7.64 us
  between operations: 14.4 us -> 0.65 us
  matrix products: 13.2 us -> 0 us
  other arithmetic: 12.6 us -> 1.38 us
    pallas_call x0 -> x1, Pallas kernels: none -> 96.3 us  [local_grads(): pl.pallas_call(local_grads_kernel, out_shape=[jax.ShapeDtypeStruct((8, TO...]
    reduce_scatter x1 -> x0, waiting for transfers between devices: 78.6 us -> none  [local(): lax.psum_scatter(contract(cycle_grad, user_low, 0, 0), 'group', scatter_d...]
    all_gather x1 -> x0, waiting for transfers between devices: 40.5 us -> none  [local(): lax.all_gather(item_low, 'group', axis=0, tiled=True)]
    all_to_all x3 -> x0, starting transfers between devices: 33.4 us -> none  [the longest x1 17 us: local(): lax.all_to_all(wanted.reshape(owner_count, capacity), 'dev', split_axis=0...]
    all_gather x1 -> x0, blocking collectives: 25.8 us -> none  [local(): lax.all_gather(item_ids, 'group', axis=0, tiled=True)]
    gather x4 -> x0, local copies, waits for them, and re-layouts: 21.4 us -> none  [the longest x1 9.43 us: local(): corpus_inv[safe_rows]]
    dot_general x13 -> x0, matrix products: 13.2 us -> none  [the longest x6 8.17 us: contract(): lax.dot_general(left, right, (((left_dim,), (right_dim,)), ((), ())), pre...]
    all_to_all x3 -> x0, waiting for transfers between devices: 10.4 us -> none  [the longest x1 10.4 us: local(): lax.all_to_all(wanted.reshape(owner_count, capacity), 'dev', split_axis=0...]
  transfers between devices with their start and end apart: 5 -> 0, of which waited for: 3 -> 0; matrix products, arithmetic and copies ran while one was open for 9% -> 0% of each run, Pallas kernels for 0% -> 0%
where the time goes in v2:
time: 158 us
  Pallas kernels  148 us (94%)
  local copies, waits for them, and re-layouts  7.64 us (5%)
    pallas_call x1, Pallas kernels, local_grads(): pl.pallas_call(local_grads_kernel, out_shape=[jax.ShapeDtypeStruct((8, TO...  96.3 us
    pallas_call x1, Pallas kernels, reduce_all(): pl.pallas_call(reduce_all_kernel, out_shape=jax.ShapeDtypeStruct((2, HALF...  51.6 us
    unnamed x10, local copies, waits for them, and re-layouts  5.02 us

profile of v2, /device:TPU:1, one launch (start us, length us, event | category | flops | bytes accessed | tf_op | source)
XLA Modules:
  0.0 157.6 jit_solution(7205900655253343427)
XLA Ops:
  0.6 0.7 broadcast_multiply_fusion
  1.3 0.7 add_bitcast_fusion
  2.0 0.7 broadcast_in_dim.2.ids_in
  2.7 0.0 copy-start
  2.7 1.0 copy-done
  3.7 0.0 copy-start.1
  3.7 1.0 copy-done.1
  4.8 0.0 copy-start.2
  4.8 1.0 copy-done.2
  5.8 0.0 copy-start.3
  5.8 0.9 copy-done.3
  6.7 0.0 copy-start.4
  6.7 0.9 copy-done.4
  7.7 96.3 %local_grads.1 = (f32[8,128]{1,0:T(8,128)S(1)}, f32[1024,256]{1,0:T(8,128)S(1)}, f32[1024,256]{1,0:T(8,128)S(1)}) custom-call(bf16[128,1024]{1,0:T(8,128)(2,1)S(1)} %copy-done.3, bf16[128,1024]{1,0:T(8,128)(2,1)S(1)} %copy-done.4, bf16[256,1024]{1,0:T(8,128)(2,1)S(1)} %copy-done, bf16[1024,256]{1,0:T(8,128)(2,1)S(1)} %copy-done.1, ...), custom_call_target="tpu_custom_call" | custom-call | tf_op jit(solution)/shard_map/local_grads/pallas_call | solution.py:486
  104.0 0.5 slice_bitcast_fusion.2
  104.5 51.6 %reduce_all.1 = f32[2,1024,256]{2,1,0:T(8,128)S(1)} custom-call(f32[1024,256]{1,0:T(8,128)S(1)} %get-tuple-element.7.user_ref, f32[1024,256]{1,0:T(8,128)S(1)} %get-tuple-element.8.item_ref), custom_call_target="tpu_custom_call" | custom-call | tf_op jit(solution)/shard_map/reduce_all/pallas_call | solution.py:180
  156.1 1.5 slice_bitcast_fusion
  (1 shorter events, 0.0 us)
Async XLA Ops:
  2.7 1.0 copy-start
  3.7 1.0 copy-start.1
  4.8 1.0 copy-start.2
  5.8 0.9 copy-start.3
  6.7 0.9 copy-start.4

commit v3 on v2

v3 whole, which is shorter than its diff:
```python
import jax
import jax.numpy as jnp
from jax import lax
from jax.experimental import pallas as pl
from jax.experimental.pallas import tpu as pltpu
from jax.sharding import PartitionSpec as P

sharpen = 20.0
epsilon = 1e-06
MESH = pl.DeviceIdType.MESH
NX, NY, NZ = 4, 4, 16


def place():
    group, dev = lax.axis_index("group"), lax.axis_index("dev")
    core, x, y_hi = group % 2, (group // 2) % NX, group // (2 * NX)
    z, y_lo = dev // 2, dev % 2
    return core, x, y_hi * 2 + y_lo, z


def device_at(core, x, y, z):
    return (((y // 2) * NX + x) * 2 + core, z * 2 + y % 2)


def greet(partners):
    barrier = pltpu.get_barrier_semaphore()
    for partner in partners:
        pl.semaphore_signal(barrier, inc=1, device_id=partner, device_id_type=MESH)
    pl.semaphore_wait(barrier, len(partners))


def remote(src, dst, send_sem, recv_sem, device):
    return pltpu.make_async_remote_copy(
        src_ref=src, dst_ref=dst, send_sem=send_sem, recv_sem=recv_sem, device_id=device, device_id_type=MESH
    )


TOK, OWN, NEG, WIDE, E = 128, 256, 512, 1024, 256
NG, ND = 16, 32
f32, bf16 = jnp.float32, jnp.bfloat16


def dot(left, right, left_dim=1, right_dim=0):
    return lax.dot_general(left, right, (((left_dim,), (right_dim,)), ((), ())), preferred_element_type=f32)


def project(features, weight):
    hidden = dot(features, weight)
    inverse = lax.rsqrt(jnp.sum(hidden * hidden, axis=-1, keepdims=True) + epsilon)
    return hidden * inverse, inverse


def unnormalize(unit, inverse, upstream):
    along = jnp.sum(unit * upstream, axis=-1, keepdims=True)
    return ((upstream - unit * along) * inverse).astype(bf16)


FOLD = 512
PART = 128
BIT = 32


def step_kernel(
    user_feat, item_feat, corpus_feat, user_weight, item_weight, ids_in, owner_in, row_in,
    loss_ref, out_ref,
    uf, itf, cf, uw, iw, ids_own, owner_own, row_own, corp, gus, cyc, ids, codes, pair_codes, tot_g, tot_d,
    select, sel_out, sel_in, cexp, sums, own_sums, unit_u, unit_i, unit_c, inv_u, inv_i, inv_c, upward, owned,
    mine, from_core, from_first, from_second, from_z,
    load_sem, ids_send, ids_recv, codes_send, codes_recv, pair_send, pair_recv, tg_send, tg_recv, td_send, td_recv,
    zc_send, zc_recv, zu_send, zu_recv, yu_send, yu_recv, ys_send, ys_recv,
    yh_send, yh_recv, x_send, x_recv, c_send, c_recv,
    core_send, core_recv, first_send, first_recv, second_send, second_recv, z_sends, z_recvs,
    zg_send, zg_recv, sg_send, sg_recv, fg_send, fg_recv, cg_send, cg_recv,
):
    core, x, y, z = place()
    y_hi, y_lo = y // 2, y % 2
    group, dev = lax.axis_index("group"), lax.axis_index("dev")
    factor = sharpen / TOK
    loads = [
        pltpu.make_async_copy(src, dst, load_sem.at[n])
        for n, (src, dst) in enumerate([
            (corpus_feat, cf), (item_weight, iw), (user_feat, uf), (user_weight, uw), (item_feat, itf),
            (ids_in, ids_own), (owner_in, owner_own), (row_in, row_own),
        ])
    ]
    for load in loads:
        load.start()
    group_peers = [(lax.rem(group + k, NG), dev) for k in range(1, NG)]
    dev_peers = [(group, lax.rem(dev + k, ND)) for k in range(1, ND)]
    sibling = device_at(1 - core, x, y, z)
    y_partner = device_at(core, x, y_hi * 2 + 1 - y_lo, z)
    y_far = device_at(core, x, (1 - y_hi) * 2 + y_lo, z)
    x_peers = [device_at(core, (x + k) % NX, y, z) for k in range(1, NX)]
    y_peers = [device_at(core, x, (y + k) % NY, z) for k in range(1, NY)]
    z_all = [device_at(core, x, y, (z + k) % NZ) for k in range(1, NZ)]
    z_peers = [z_all[0], z_all[-1]]
    sends = []

    def send(src, dst, send_sem, recv_sem, device):
        copy = remote(src, dst, send_sem, recv_sem, device)
        copy.start()
        sends.append(copy)

    def arrived(dst, send_sem, recv_sem, device):
        remote(dst, dst, send_sem, recv_sem, device).wait_recv()

    barrier = pltpu.get_barrier_semaphore()
    greeted = group_peers + dev_peers + [device_at(core, x, NY - 1 - y, z)]
    for partner in greeted:
        pl.semaphore_signal(barrier, inc=1, device_id=partner, device_id_type=MESH)

    first_at, second_at = [x, y], [y, x]
    along = [x_peers, y_peers]

    def part_rows(fold, part):
        return pl.ds(pl.multiple_of(fold * FOLD + part * PART, PART), PART)

    def bit_rows(fold, part, bit):
        return pl.ds(pl.multiple_of(fold * FOLD + part * PART + bit * BIT, BIT), BIT)

    def tile_of(at):
        fold = at // 8
        row = fold * FOLD + (x + fold * (y - x)) * PART + (y + fold * (x - y)) * BIT + ((at // 2) % 4) * 8
        return pl.ds(pl.multiple_of(row, 8), 8), pl.ds(pl.multiple_of((at % 2) * 128, 128), 128)

    order = [(k, fold) for k in (1, 2, 3, 0) for fold in (0, 1)]
    far_order = [(k, fold) for k in (1, 2, 3) for fold in (0, 1)]

    def order_rows(n):
        k, fold = order[n]
        return part_rows(fold, (first_at[fold] + k) % 4)

    def core_copy(q, n):
        return remote(mine.at[q, order_rows(n)], from_core.at[n], core_send.at[n], core_recv.at[n], sibling)

    def first_copy(q, k, fold):
        rows = part_rows(fold, (first_at[fold] + k) % 4)
        return remote(
            mine.at[q, rows], from_first.at[fold, k - 1], first_send.at[fold, k - 1], first_recv.at[fold, k - 1],
            along[fold][k - 1],
        )

    def second_copy(q, k, fold):
        rows = bit_rows(fold, first_at[fold], (second_at[fold] + k) % 4)
        return remote(
            mine.at[q, rows], from_second.at[fold, k - 1], second_send.at[fold, k - 1], second_recv.at[fold, k - 1],
            along[1 - fold][k - 1],
        )

    def z_copy(q, k):
        rows, columns = tile_of((z + k) % NZ)
        return remote(mine.at[q, rows, columns], from_z.at[k - 1], z_sends.at[k - 1], z_recvs.at[k - 1], z_all[k - 1])

    def zg_copy(q, k, back):
        rows, columns = tile_of((z + NZ - k * back) % NZ)
        tile = out_ref.at[q, rows, columns]
        return remote(tile, tile, zg_send.at[k - 1], zg_recv.at[k - 1], z_all[k - 1])

    def sg_copy(q, k, fold, back):
        bit = out_ref.at[q, bit_rows(fold, first_at[fold], (second_at[fold] + 4 - k * back) % 4)]
        return remote(bit, bit, sg_send.at[fold, k - 1], sg_recv.at[fold, k - 1], along[1 - fold][k - 1])

    def fg_copy(q, k, fold, back):
        part = out_ref.at[q, part_rows(fold, (first_at[fold] + 4 - k * back) % 4)]
        return remote(part, part, fg_send.at[fold, k - 1], fg_recv.at[fold, k - 1], along[fold][k - 1])

    def cg_copy(q, k, fold):
        part = out_ref.at[q, part_rows(fold, (first_at[fold] + 4 - k) % 4)]
        return remote(part, part, cg_send.at[fold, k], cg_recv.at[fold, k], sibling)

    def reduce_first(q):
        for n, (k, fold) in enumerate(order):
            rows = order_rows(n)
            core_copy(q, n).wait_recv()
            mine[q, rows] += from_core[n]
            if k:
                first_copy(q, k, fold).start()

    def reduce_second(q):
        for k, fold in far_order:
            first_copy(q, k, fold).wait_recv()
        for k, fold in order:
            at = (second_at[fold] + k) % 4
            rows = bit_rows(fold, first_at[fold], at)
            near = pl.ds(pl.multiple_of(at * BIT, BIT), BIT)
            mine[q, rows] += from_first[fold, 0, near] + from_first[fold, 1, near] + from_first[fold, 2, near]
            if k:
                second_copy(q, k, fold).start()

    def reduce_z(q):
        for k, fold in far_order:
            second_copy(q, k, fold).wait_recv()
        for fold in (0, 1):
            rows = bit_rows(fold, first_at[fold], second_at[fold])
            mine[q, rows] += from_second[fold, 0] + from_second[fold, 1] + from_second[fold, 2]
        for k in range(1, NZ):
            z_copy(q, k).start()

    def gather_z(q):
        rows, columns = tile_of(z)
        total = mine[q, rows, columns]
        for k in range(1, NZ):
            z_copy(q, k).wait_recv()
            total = total + from_z[k - 1]
        out_ref[q, rows, columns] = total
        for k in range(1, NZ):
            zg_copy(q, k, 0).start()

    def gather_rest(q):
        for k in range(1, NZ):
            zg_copy(q, k, 1).wait_recv()
        for k, fold in far_order:
            sg_copy(q, k, fold, 0).start()
        for k, fold in far_order:
            sg_copy(q, k, fold, 1).wait_recv()
        for k, fold in far_order:
            fg_copy(q, k, fold, 0).start()
        for fold in (0, 1):
            cg_copy(q, 0, fold).start()
        for k, fold in far_order:
            fg_copy(q, k, fold, 1).wait_recv()
            cg_copy(q, k, fold).start()
        for k, fold in far_order:
            first_copy(q, k, fold).wait_send()
            second_copy(q, k, fold).wait_send()
            sg_copy(q, k, fold, 0).wait_send()
            fg_copy(q, k, fold, 0).wait_send()
        for k in range(1, NZ):
            z_copy(q, k).wait_send()
            zg_copy(q, k, 0).wait_send()
        for k, fold in order:
            cg_copy(q, k, fold).wait_send()

    def take_gathered(q):
        for k, fold in order:
            cg_copy(q, k, fold).wait_recv()
        for n in range(len(order)):
            core_copy(q, n).wait_send()

    def on_core(which, action, *given):
        @pl.when(core == which)
        def _():
            action(*given)

    loads[0].wait()
    loads[1].wait()
    unit, inverse = project(cf[...], iw[...])
    unit_c[...] = unit
    inv_c[...] = inverse
    corp[z] = unit.astype(bf16).reshape(2, TOK, E)
    pl.semaphore_wait(barrier, len(greeted))

    def z_send(buf, at, s, e, way, send_sem, recv_sem):
        send(buf.at[at, e], buf.at[at, e], send_sem.at[way, s - 1, e], recv_sem.at[way, s - 1, e], z_peers[way])

    def source(way, s):
        return (z + NZ - s) % NZ if way == 0 else (z + s) % NZ

    def z_step(buf, s, send_sem, recv_sem, work=()):
        work = list(work)
        for e in (0, 1):
            for way in (0, 1):
                if s == 8 and e != way:
                    continue
                at = source(way, s)
                arrived(buf.at[at, e], send_sem.at[way, s - 1, e], recv_sem.at[way, s - 1, e], z_peers[way])
                if s < 7 or (s == 7 and e == way):
                    z_send(buf, at, s + 1, e, way, send_sem, recv_sem)
                if work:
                    work.pop(0)()
        for piece in work:
            piece()

    for e in (0, 1):
        for way in (0, 1):
            z_send(corp, z, 1, e, way, zc_send, zc_recv)
    for load in loads[5:]:
        load.wait()
    code = owner_own[...] * OWN + row_own[...]
    codes[dev] = jnp.concatenate([code, code], axis=0)
    ids[group] = jnp.broadcast_to(ids_own[...], (8, TOK))
    send(codes.at[dev], pair_codes, pair_send, pair_recv, y_partner)

    loads[2].wait()
    loads[3].wait()
    unit, inverse = project(uf[...], uw[...])
    unit_u[...] = unit
    inv_u[...] = inverse
    user_low = unit.astype(bf16)
    cyc[group, 0] = user_low
    gus[z, y_lo] = user_low
    loads[4].wait()
    unit, inverse = project(itf[...], iw[...])
    unit_i[...] = unit
    inv_i[...] = inverse
    item_low = unit.astype(bf16)
    cyc[group, 1] = item_low
    far_group = lax.rem(group + NG // 2, NG)
    send(cyc.at[group], cyc.at[group], yh_send, yh_recv, y_far)
    for k in range(1, NX):
        send(cyc.at[group], cyc.at[group], x_send.at[0, k - 1], x_recv.at[0, k - 1], x_peers[k - 1])
    send(gus.at[z, y_lo], gus.at[z, y_lo], yu_send, yu_recv, y_partner)
    send(cyc.at[group], cyc.at[group], c_send.at[0, 0], c_recv.at[0, 0], sibling)

    def group_of(far, k, other):
        row = y_hi + far * (1 - 2 * y_hi)
        return (row * NX + (x + NX - k) % NX) * 2 + core + other * (1 - 2 * core)

    arrived(pair_codes, pair_send, pair_recv, y_partner)
    own_codes, their_codes = codes[dev], pair_codes[...]
    code_row = jnp.concatenate(
        [own_codes[n : n + 1] for n in range(4)] + [their_codes[n : n + 1] for n in range(4)], axis=1
    )
    wide_rows = lax.broadcasted_iota(jnp.int32, (OWN, 2 * NEG), 0)

    def select_from(at):
        hot = (code_row - (at * 2 + y_lo) * OWN == wide_rows).astype(f32).astype(bf16)
        return dot(corp[at].reshape(OWN, E), hot, 0, 0)

    def nothing():
        pass

    def select_more(way, s):
        def piece():
            select[...] += select_from(source(way, s))

        return piece

    select[...] = select_from(z)
    for s in range(1, 9):
        work = [nothing, select_more(0, s - 1), nothing, select_more(1, s - 1)] if s > 1 else []
        z_step(corp, s, zc_send, zc_recv, work)
        if s == 1:
            for k in range(1, ND):
                send(codes.at[dev], codes.at[dev], codes_send.at[k - 1], codes_recv.at[k - 1], dev_peers[k - 1])
        if s == 2:
            arrived(cyc.at[far_group], yh_send, yh_recv, y_far)
            for k in range(1, NX):
                send(cyc.at[far_group], cyc.at[far_group], x_send.at[1, k - 1], x_recv.at[1, k - 1], x_peers[k - 1])
            send(cyc.at[far_group], cyc.at[far_group], c_send.at[1, 0], c_recv.at[1, 0], sibling)
        if s == 3:
            for k in range(1, NG):
                send(ids.at[group], ids.at[group], ids_send.at[k - 1], ids_recv.at[k - 1], group_peers[k - 1])
        if s in (4, 6):
            far = (s - 4) // 2
            for k in range(1, NX):
                block = cyc.at[group_of(far, k, 0)]
                arrived(block, x_send.at[far, k - 1], x_recv.at[far, k - 1], x_peers[k - 1])
                send(block, block, c_send.at[far, k], c_recv.at[far, k], sibling)
        if s == 7:
            arrived(gus.at[z, 1 - y_lo], yu_send, yu_recv, y_partner)
            for e in (0, 1):
                for way in (0, 1):
                    z_send(gus, z, 1, e, way, zu_send, zu_recv)
    select[...] += select_from(source(0, 8))
    sel_out[...] = select[:, NEG:].astype(bf16)
    send(sel_out, sel_in, ys_send, ys_recv, y_partner)

    for far in (0, 1):
        for k in range(NX):
            arrived(cyc.at[group_of(far, k, 1)], c_send.at[far, k], c_recv.at[far, k], sibling)
    for k in range(1, NG):
        arrived(ids.at[lax.rem(group + NG - k, NG)], ids_send.at[k - 1], ids_recv.at[k - 1], group_peers[k - 1])

    tile_rows = lax.broadcasted_iota(jnp.int32, (TOK, TOK), 0)
    tile_columns = lax.broadcasted_iota(jnp.int32, (TOK, TOK), 1)
    eye = tile_rows == tile_columns

    def to_row(column):
        return jnp.sum(jnp.where(eye, column, 0.0), axis=0, keepdims=True)

    own_ids = ids_own[...].astype(f32)
    ids_column = jnp.sum(jnp.where(eye, own_ids, 0.0), axis=1, keepdims=True)
    user_low = cyc[group, 0]
    item_low = cyc[group, 1]

    def masks(g):
        diagonal = tile_columns + g * TOK == tile_rows + group * TOK
        same = ids[g, 0:1].astype(f32) == ids_column
        return diagonal, jnp.logical_and(same, jnp.logical_not(diagonal))

    def cycle_forward(g, carry):
        logit = sharpen * dot(user_low, cyc[g, 1], 1, 1)
        diagonal, hidden = masks(g)
        value = jnp.where(hidden, 0.0, jnp.exp(logit))
        cexp[g] = value
        return carry[0] + value, carry[1] + jnp.where(diagonal, logit, 0.0)

    def forward_piece(n):
        def piece():
            sums[...], own_sums[...] = lax.fori_loop(
                4 * n, 4 * n + 4, cycle_forward, (sums[...], own_sums[...]), unroll=2
            )

        return piece

    sums[...] = jnp.zeros((TOK, TOK), f32)
    own_sums[...] = jnp.zeros((TOK, TOK), f32)
    z_step(gus, 1, zu_send, zu_recv, [forward_piece(n) for n in range(4)])
    arrived(sel_in, ys_send, ys_recv, y_partner)
    sample_low = (select[:, :NEG] + sel_in[...].astype(f32)).astype(bf16)
    sample_exp = jnp.exp(sharpen * dot(user_low, sample_low))
    total = jnp.sum(sums[...], axis=1, keepdims=True) + jnp.sum(sample_exp, axis=1, keepdims=True)
    total_row = to_row(total)
    tot_g[group] = jnp.broadcast_to(total_row, (8, TOK))
    tot_d[dev] = jnp.broadcast_to(total_row, (8, TOK))
    for k in range(1, ND):
        send(tot_d.at[dev], tot_d.at[dev], td_send.at[k - 1], td_recv.at[k - 1], dev_peers[k - 1])
    for k in range(1, NG):
        send(tot_g.at[group], tot_g.at[group], tg_send.at[k - 1], tg_recv.at[k - 1], group_peers[k - 1])
    own_logit = jnp.sum(own_sums[...], axis=1, keepdims=True)
    loss_ref[...] = jnp.broadcast_to(to_row(jnp.log(total) - own_logit), (8, TOK))
    inverse_total = 1.0 / total
    sample_grad = (sample_exp * inverse_total * factor).astype(bf16)

    def user_backward(g, up):
        diagonal = tile_columns + g * TOK == tile_rows + group * TOK
        grad = ((cexp[g] * inverse_total - diagonal.astype(f32)) * factor).astype(bf16)
        return up + dot(grad, cyc[g, 1])

    def user_piece(n):
        def piece():
            start = upward[...] if n else dot(sample_grad, sample_low, 1, 1)
            upward[...] = lax.fori_loop(4 * n, 4 * n + 4, user_backward, start, unroll=2)

        return piece

    z_step(gus, 2, zu_send, zu_recv, [user_piece(n) for n in range(4)])
    user_back = unnormalize(unit_u[...], inv_u[...], upward[...])

    def user_part(n):
        rows = order_rows(n)
        mine[0, rows] = dot(uf[:, rows], user_back, 0, 0)
        on_core(1, lambda: core_copy(0, n).start())

    def user_parts(n):
        def piece():
            user_part(2 * n)
            user_part(2 * n + 1)

        return piece

    z_step(gus, 3, zu_send, zu_recv, [user_parts(n) for n in range(4)])
    for k in range(1, NG):
        arrived(tot_g.at[lax.rem(group + NG - k, NG)], tg_send.at[k - 1], tg_recv.at[k - 1], group_peers[k - 1])

    def item_backward(g, up):
        users = cyc[g, 0]
        diagonal, hidden = masks(g)
        value = jnp.where(hidden, 0.0, jnp.exp(sharpen * dot(item_low, users, 1, 1)))
        grad = ((value * (1.0 / tot_g[g, 0:1]) - diagonal.astype(f32)) * factor).astype(bf16)
        return up + dot(grad, users)

    def item_piece(n):
        def piece():
            start = upward[...] if n else jnp.zeros((TOK, E), f32)
            upward[...] = lax.fori_loop(4 * n, 4 * n + 4, item_backward, start, unroll=2)

        return piece

    z_step(gus, 4, zu_send, zu_recv, [item_piece(n) for n in range(4)])
    item_back = unnormalize(unit_i[...], inv_i[...], upward[...])
    mine[1] = dot(itf[...], item_back, 0, 0)
    on_core(0, reduce_first, 0)
    for k in range(1, ND):
        at = lax.rem(dev + ND - k, ND)
        arrived(codes.at[at], codes_send.at[k - 1], codes_recv.at[k - 1], dev_peers[k - 1])
        arrived(tot_d.at[at], td_send.at[k - 1], td_recv.at[k - 1], dev_peers[k - 1])
    owned[...] = jnp.zeros((OWN, E), f32)
    corpus_low = corp[z].reshape(OWN, E)
    code_rows = lax.broadcasted_iota(jnp.int32, (OWN, NEG), 0)
    ones = jnp.ones((NEG, 128), bf16)

    def corpus_backward(j, carry):
        s = (j + 2) // 4
        at = (z + NZ - s + 2 * s * (((j + 2) % 4) // 2)) % NZ
        e = j % 2
        users = gus[at, e]
        holder = at * 2 + e
        value = jnp.exp(sharpen * dot(corpus_low, users, 1, 1))
        grad = (value * (1.0 / tot_d[holder, 0:1]) * factor).astype(bf16)
        back = unnormalize(unit_c[...], inv_c[...], dot(grad, users)).astype(f32)
        named = codes[holder]
        row = jnp.concatenate([named[n : n + 1] for n in range(4)], axis=1)
        hot = (row - dev * OWN == code_rows).astype(f32).astype(bf16)
        count = dot(hot, ones)
        owned[...] += jnp.concatenate([count, count], axis=1) * back
        return carry

    def corpus_piece(first, last):
        return lambda: lax.fori_loop(first, last, corpus_backward, 0)

    z_step(gus, 5, zu_send, zu_recv, [corpus_piece(3 * n, 3 * n + 3) for n in range(4)])
    on_core(0, reduce_second, 0)
    z_step(gus, 6, zu_send, zu_recv, [corpus_piece(12 + 2 * n, 14 + 2 * n) for n in range(4)])
    on_core(0, reduce_z, 0)
    z_step(gus, 7, zu_send, zu_recv, [corpus_piece(20, 22), corpus_piece(22, 24), corpus_piece(24, 26)])
    z_step(gus, 8, zu_send, zu_recv, [corpus_piece(26, 28), corpus_piece(28, 30)])
    corpus_piece(30, 32)()
    high = owned[...].astype(bf16)
    low = (owned[...] - high.astype(f32)).astype(bf16)
    for n in range(len(order)):
        rows = order_rows(n)
        mine[1, rows] += dot(cf[:, rows], high, 0, 0) + dot(cf[:, rows], low, 0, 0)
        on_core(0, lambda: core_copy(1, n).start())
    on_core(1, reduce_first, 1)
    on_core(1, reduce_second, 1)
    on_core(1, reduce_z, 1)
    on_core(1, gather_z, 1)
    on_core(1, gather_rest, 1)
    on_core(0, gather_z, 0)
    on_core(0, gather_rest, 0)
    on_core(1, take_gathered, 0)
    on_core(0, take_gathered, 1)
    for copy in sends:
        copy.wait_send()


def step(user_feat, item_feat, corpus_feat, user_weight, item_weight, ids, owners, rows):
    dma, vmem = pltpu.SemaphoreType.DMA, pltpu.VMEM
    pairs = lambda *shape: [dma(shape), dma(shape)]
    return pl.pallas_call(
        step_kernel,
        out_shape=[jax.ShapeDtypeStruct((8, TOK), f32), jax.ShapeDtypeStruct((2, WIDE, E), f32)],
        in_specs=[pl.BlockSpec(memory_space=pl.ANY)] * 8,
        out_specs=[pl.BlockSpec(memory_space=pltpu.VMEM)] * 2,
        scratch_shapes=[
            vmem((TOK, WIDE), bf16), vmem((TOK, WIDE), bf16), vmem((OWN, WIDE), bf16),
            vmem((WIDE, E), bf16), vmem((WIDE, E), bf16),
            vmem((1, TOK), jnp.int32), vmem((4, 128), jnp.int32), vmem((4, 128), jnp.int32),
            vmem((NZ, 2, TOK, E), bf16), vmem((NZ, 2, TOK, E), bf16), vmem((NG, 2, TOK, E), bf16),
            vmem((NG, 8, 128), jnp.int32), vmem((ND, 8, 128), jnp.int32), vmem((8, 128), jnp.int32),
            vmem((NG, 8, 128), f32), vmem((ND, 8, 128), f32),
            vmem((E, 2 * NEG), f32), vmem((E, NEG), bf16), vmem((E, NEG), bf16), vmem((NG, TOK, TOK), f32),
            vmem((TOK, TOK), f32), vmem((TOK, TOK), f32),
            vmem((TOK, E), f32), vmem((TOK, E), f32), vmem((OWN, E), f32),
            vmem((TOK, 1), f32), vmem((TOK, 1), f32), vmem((OWN, 1), f32), vmem((TOK, E), f32), vmem((OWN, E), f32),
            vmem((2, WIDE, E), f32), vmem((8, PART, E), f32), vmem((2, 3, PART, E), f32), vmem((2, 3, BIT, E), f32),
            vmem((NZ - 1, 8, 128), f32),
            dma((8,)), *pairs(NG - 1), *pairs(ND - 1), *pairs(), *pairs(NG - 1), *pairs(ND - 1),
            *pairs(2, 8, 2), *pairs(2, 8, 2), *pairs(), *pairs(), *pairs(), *pairs(2, 3), *pairs(2, 4),
            *pairs(8), *pairs(2, 3), *pairs(2, 3), *pairs(NZ - 1), *pairs(NZ - 1), *pairs(2, 3), *pairs(2, 3),
            *pairs(2, 4),
        ],
        compiler_params=pltpu.CompilerParams(
            collective_id=0, has_side_effects=True, vmem_limit_bytes=60 * 1024 * 1024
        ),
        name="step",
    )(user_feat, item_feat, corpus_feat, user_weight, item_weight, ids, owners, rows)


def local(
    user_feat, item_feat, item_ids, corpus_feat, neg_owner, neg_row, user_weight, item_weight
):
    loss, grads = step(
        user_feat, item_feat, corpus_feat, user_weight, item_weight,
        item_ids.reshape(1, TOK), neg_owner.reshape(4, 128), neg_row.reshape(4, 128),
    )
    return loss[0], grads[0], grads[1]


def solution(mesh):
    return jax.shard_map(
        local,
        mesh=mesh,
        in_specs=(
            P(("group", "dev"), None),
            P(("group", "dev"), None),
            P(("group", "dev")),
            P(("group", "dev"), None),
            P(("group", "dev"), None),
            P(("group", "dev")),
            P(),
            P(),
        ),
        out_specs=(P(("group", "dev")), P(), P()),
        check_vma=False,
    )
```

time: 158 us -> 140 us (0.89)
  Pallas kernels: 148 us -> 135 us
  local copies, waits for them, and re-layouts: 7.64 us -> 4.18 us
    pallas_call x2 -> x1, Pallas kernels: 148 us -> 135 us  [step(): pl.pallas_call(step_kernel, out_shape=[jax.ShapeDtypeStruct((8, TOK), f32...]
    unnamed x10 -> x0, local copies, waits for them, and re-layouts: 5.02 us -> none
    squeeze x2, local copies, waits for them, and re-layouts: 1.96 us -> 4.18 us  [local(): return (loss[0], grads[0], grads[1])]
where the time goes in v3:
time: 140 us
  Pallas kernels  135 us (96%)
  local copies, waits for them, and re-layouts  4.18 us (3%)
    pallas_call x1, Pallas kernels, step(): pl.pallas_call(step_kernel, out_shape=[jax.ShapeDtypeStruct((8, TOK), f32...  135 us
    squeeze x2, local copies, waits for them, and re-layouts, local(): return (loss[0], grads[0], grads[1])  4.18 us

profile of v3, /device:TPU:1, one launch (start us, length us, event | category | flops | bytes accessed | tf_op | source)
XLA Modules:
  0.0 140.1 jit_solution(8515117353197958495)
XLA Ops:
  0.6 135.3 %step.1 = (f32[8,128]{1,0:T(8,128)}, f32[2,1024,256]{2,1,0:T(8,128)}) custom-call(bf16[128,1024]{1,0:T(8,128)(2,1)} %user_feat.1, bf16[128,1024]{1,0:T(8,128)(2,1)} %item_feat.1, bf16[256,1024]{1,0:T(8,128)(2,1)} %corpus_feat.1, bf16[1024,256]{1,0:T(8,128)(2,1)} %user_weight.1, bf16[1024,256]{1,0:T(8,128)(2,1)} %item_weight.1, s32[1,128]{1,0:T(1,128)} %bitcast.11, ...), custom_call_target="tpu_custom_call" | custom-call | tf_op jit(solution)/shard_map/step/pallas_call | solution.py:522
  135.9 1.2 slice_bitcast_fusion.2
  137.1 3.0 %slice_bitcast_fusion = (f32[1024,256]{1,0:T(8,128)}, f32[1024,256]{1,0:T(8,128)}) fusion(f32[2,1024,256]{2,1,0:T(8,128)} %get-tuple-element.6), kind=kLoop, calls=%fused_computation | loop fusion | bytes 4194304 | tf_op jit(solution)/shard_map/squeeze | solution.py:559

commit v4 on v3

--- a/solution.py
+++ b/solution.py
@@ -37,6 +37,7 @@
 
 TOK, OWN, NEG, WIDE, E = 128, 256, 512, 1024, 256
 NG, ND = 16, 32
+QUAD = 4
 f32, bf16 = jnp.float32, jnp.bfloat16
 
 
@@ -64,7 +65,7 @@
     user_feat, item_feat, corpus_feat, user_weight, item_weight, ids_in, owner_in, row_in,
     loss_ref, out_ref,
     uf, itf, cf, uw, iw, ids_own, owner_own, row_own, corp, gus, cyc, ids, codes, pair_codes, tot_g, tot_d,
-    select, sel_out, sel_in, cexp, sums, own_sums, unit_u, unit_i, unit_c, inv_u, inv_i, inv_c, upward, owned,
+    select, sel_out, sel_in, cexp, counts, sums, own_sums, unit_u, unit_i, unit_c, inv_u, inv_i, inv_c, upward, owned,
     mine, from_core, from_first, from_second, from_z,
     load_sem, ids_send, ids_recv, codes_send, codes_recv, pair_send, pair_recv, tg_send, tg_recv, td_send, td_recv,
     zc_send, zc_recv, zu_send, zu_recv, yu_send, yu_recv, ys_send, ys_recv,
@@ -326,9 +327,24 @@
 
         return piece
 
+    code_rows = lax.broadcasted_iota(jnp.int32, (OWN, NEG), 0) + dev * OWN
+    ones = jnp.ones((NEG, 128), bf16)
+
+    def count_named(holder, carry):
+        named = codes[holder]
+        row = jnp.concatenate([named[n : n + 1] for n in range(4)], axis=1)
+        counts[holder] = dot((row == code_rows).astype(f32).astype(bf16), ones).astype(bf16)
+        return carry
+
+    def count_piece(first, last):
+        return lambda: lax.fori_loop(first, last, count_named, 0, unroll=2)
+
     select[...] = select_from(z)
     for s in range(1, 9):
         work = [nothing, select_more(0, s - 1), nothing, select_more(1, s - 1)] if s > 1 else []
+        if 5 <= s <= 7:
+            work[0] = count_piece(12 * s - 60, 12 * s - 54)
+            work[2] = count_piece(12 * s - 54, min(12 * s - 48, ND))
         z_step(corp, s, zc_send, zc_recv, work)
         if s == 1:
             for k in range(1, ND):
@@ -347,6 +363,10 @@
                 block = cyc.at[group_of(far, k, 0)]
                 arrived(block, x_send.at[far, k - 1], x_recv.at[far, k - 1], x_peers[k - 1])
                 send(block, block, c_send.at[far, k], c_recv.at[far, k], sibling)
+        if s == 4:
+            for k in range(1, ND):
+                at = lax.rem(dev + ND - k, ND)
+                arrived(codes.at[at], codes_send.at[k - 1], codes_recv.at[k - 1], dev_peers[k - 1])
         if s == 7:
             arrived(gus.at[z, 1 - y_lo], yu_send, yu_recv, y_partner)
             for e in (0, 1):
@@ -374,23 +394,34 @@
     user_low = cyc[group, 0]
     item_low = cyc[group, 1]
 
-    def masks(g):
-        diagonal = tile_columns + g * TOK == tile_rows + group * TOK
-        same = ids[g, 0:1].astype(f32) == ids_column
+    wide_columns = lax.broadcasted_iota(jnp.int32, (TOK, QUAD * TOK), 1)
+    own_column = lax.broadcasted_iota(jnp.int32, (TOK, QUAD * TOK), 0) + group * TOK
+
+    def side(n, which):
+        return cyc[QUAD * n : QUAD * n + QUAD, which].reshape(QUAD * TOK, E)
+
+    def row_of(tiles, n):
+        return jnp.concatenate([tiles[QUAD * n + i, 0:1] for i in range(QUAD)], axis=1)
+
+    def diagonal_of(n):
+        return wide_columns + n * QUAD * TOK == own_column
+
+    def masks(n):
+        diagonal = diagonal_of(n)
+        same = row_of(ids, n).astype(f32) == ids_column
         return diagonal, jnp.logical_and(same, jnp.logical_not(diagonal))
 
-    def cycle_forward(g, carry):
-        logit = sharpen * dot(user_low, cyc[g, 1], 1, 1)
-        diagonal, hidden = masks(g)
-        value = jnp.where(hidden, 0.0, jnp.exp(logit))
-        cexp[g] = value
-        return carry[0] + value, carry[1] + jnp.where(diagonal, logit, 0.0)
+    def folded(wide):
+        return sum(wide[:, i * TOK : i * TOK + TOK] for i in range(QUAD))
 
     def forward_piece(n):
         def piece():
-            sums[...], own_sums[...] = lax.fori_loop(
-                4 * n, 4 * n + 4, cycle_forward, (sums[...], own_sums[...]), unroll=2
-            )
+            logit = sharpen * dot(user_low, side(n, 1), 1, 1)
+            diagonal, hidden = masks(n)
+            value = jnp.where(hidden, 0.0, jnp.exp(logit))
+            cexp[n] = value
+            sums[...] += folded(value)
+            own_sums[...] += folded(jnp.where(diagonal, logit, 0.0))
 
         return piece
 
@@ -413,15 +444,11 @@
     inverse_total = 1.0 / total
     sample_grad = (sample_exp * inverse_total * factor).astype(bf16)
 
-    def user_backward(g, up):
-        diagonal = tile_columns + g * TOK == tile_rows + group * TOK
-        grad = ((cexp[g] * inverse_total - diagonal.astype(f32)) * factor).astype(bf16)
-        return up + dot(grad, cyc[g, 1])
-
     def user_piece(n):
         def piece():
             start = upward[...] if n else dot(sample_grad, sample_low, 1, 1)
-            upward[...] = lax.fori_loop(4 * n, 4 * n + 4, user_backward, start, unroll=2)
+            grad = ((cexp[n] * inverse_total - diagonal_of(n).astype(f32)) * factor).astype(bf16)
+            upward[...] = start + dot(grad, side(n, 1))
 
         return piece
 
@@ -444,17 +471,14 @@
     for k in range(1, NG):
         arrived(tot_g.at[lax.rem(group + NG - k, NG)], tg_send.at[k - 1], tg_recv.at[k - 1], group_peers[k - 1])
 
-    def item_backward(g, up):
-        users = cyc[g, 0]
-        diagonal, hidden = masks(g)
-        value = jnp.where(hidden, 0.0, jnp.exp(sharpen * dot(item_low, users, 1, 1)))
-        grad = ((value * (1.0 / tot_g[g, 0:1]) - diagonal.astype(f32)) * factor).astype(bf16)
-        return up + dot(grad, users)
-
     def item_piece(n):
         def piece():
-            start = upward[...] if n else jnp.zeros((TOK, E), f32)
-            upward[...] = lax.fori_loop(4 * n, 4 * n + 4, item_backward, start, unroll=2)
+            users = side(n, 0)
+            diagonal, hidden = masks(n)
+            value = jnp.where(hidden, 0.0, jnp.exp(sharpen * dot(item_low, users, 1, 1)))
+            grad = ((value * (1.0 / row_of(tot_g, n)) - diagonal.astype(f32)) * factor).astype(bf16)
+            up = dot(grad, users)
+            upward[...] = upward[...] + up if n else up
 
         return piece
 
@@ -464,41 +488,38 @@
     on_core(0, reduce_first, 0)
     for k in range(1, ND):
         at = lax.rem(dev + ND - k, ND)
-        arrived(codes.at[at], codes_send.at[k - 1], codes_recv.at[k - 1], dev_peers[k - 1])
         arrived(tot_d.at[at], td_send.at[k - 1], td_recv.at[k - 1], dev_peers[k - 1])
     owned[...] = jnp.zeros((OWN, E), f32)
     corpus_low = corp[z].reshape(OWN, E)
-    code_rows = lax.broadcasted_iota(jnp.int32, (OWN, NEG), 0)
-    ones = jnp.ones((NEG, 128), bf16)
-
-    def corpus_backward(j, carry):
-        s = (j + 2) // 4
-        at = (z + NZ - s + 2 * s * (((j + 2) % 4) // 2)) % NZ
-        e = j % 2
-        users = gus[at, e]
-        holder = at * 2 + e
+
+    def corpus_backward(at):
+        users = gus[at].reshape(2 * TOK, E)
         value = jnp.exp(sharpen * dot(corpus_low, users, 1, 1))
-        grad = (value * (1.0 / tot_d[holder, 0:1]) * factor).astype(bf16)
-        back = unnormalize(unit_c[...], inv_c[...], dot(grad, users)).astype(f32)
-        named = codes[holder]
-        row = jnp.concatenate([named[n : n + 1] for n in range(4)], axis=1)
-        hot = (row - dev * OWN == code_rows).astype(f32).astype(bf16)
-        count = dot(hot, ones)
-        owned[...] += jnp.concatenate([count, count], axis=1) * back
-        return carry
-
-    def corpus_piece(first, last):
-        return lambda: lax.fori_loop(first, last, corpus_backward, 0)
-
-    z_step(gus, 5, zu_send, zu_recv, [corpus_piece(3 * n, 3 * n + 3) for n in range(4)])
+        holder = at * 2
+        scale = 1.0 / jnp.concatenate([tot_d[holder, 0:1], tot_d[holder + 1, 0:1]], axis=1)
+        named = jnp.concatenate([counts[holder], counts[holder + 1]], axis=1).astype(f32)
+        return dot((value * scale * factor * named).astype(bf16), users)
+
+    def corpus_piece(*ats):
+        def piece():
+            owned[...] += sum(corpus_backward(at) for at in ats)
+
+        return piece
+
+    def both(s):
+        return source(0, s), source(1, s)
+
+    z_step(gus, 5, zu_send, zu_recv, [corpus_piece(z, source(0, 1)), corpus_piece(source(1, 1), source(0, 2)),
+                                      corpus_piece(source(1, 2), source(0, 3)), corpus_piece(source(1, 3))])
     on_core(0, reduce_second, 0)
-    z_step(gus, 6, zu_send, zu_recv, [corpus_piece(12 + 2 * n, 14 + 2 * n) for n in range(4)])
+    z_step(gus, 6, zu_send, zu_recv, [corpus_piece(*both(4)), nothing, corpus_piece(*both(5)), nothing])
     on_core(0, reduce_z, 0)
-    z_step(gus, 7, zu_send, zu_recv, [corpus_piece(20, 22), corpus_piece(22, 24), corpus_piece(24, 26)])
-    z_step(gus, 8, zu_send, zu_recv, [corpus_piece(26, 28), corpus_piece(28, 30)])
-    corpus_piece(30, 32)()
-    high = owned[...].astype(bf16)
-    low = (owned[...] - high.astype(f32)).astype(bf16)
+    z_step(gus, 7, zu_send, zu_recv, [nothing, corpus_piece(*both(6))])
+    z_step(gus, 8, zu_send, zu_recv, [corpus_piece(*both(7))])
+    corpus_piece(source(0, 8))()
+    owned_back = (owned[...] - unit_c[...] * jnp.sum(unit_c[...] * owned[...], axis=-1, keepdims=True)) * inv_c[...]
+    high = owned_back.astype(bf16)
+    low = (owned_back - high.astype(f32)).astype(bf16)
     for n in range(len(order)):
         rows = order_rows(n)
         mine[1, rows] += dot(cf[:, rows], high, 0, 0) + dot(cf[:, rows], low, 0, 0)
@@ -531,7 +552,7 @@
             vmem((NZ, 2, TOK, E), bf16), vmem((NZ, 2, TOK, E), bf16), vmem((NG, 2, TOK, E), bf16),
             vmem((NG, 8, 128), jnp.int32), vmem((ND, 8, 128), jnp.int32), vmem((8, 128), jnp.int32),
             vmem((NG, 8, 128), f32), vmem((ND, 8, 128), f32),
-            vmem((E, 2 * NEG), f32), vmem((E, NEG), bf16), vmem((E, NEG), bf16), vmem((NG, TOK, TOK), f32),
+            vmem((E, 2 * NEG), f32), vmem((E, NEG), bf16), vmem((E, NEG), bf16), vmem((NG // QUAD, TOK, QUAD * TOK), f32), vmem((ND, OWN, 128), bf16),
             vmem((TOK, TOK), f32), vmem((TOK, TOK), f32),
             vmem((TOK, E), f32), vmem((TOK, E), f32), vmem((OWN, E), f32),
             vmem((TOK, 1), f32), vmem((TOK, 1), f32), vmem((OWN, 1), f32), vmem((TOK, E), f32), vmem((OWN, E), f32),

time: 140 us -> 138 us (0.986)
  Pallas kernels: 135 us -> 133 us
    pallas_call x1, Pallas kernels: 135 us -> 133 us  [step(): pl.pallas_call(step_kernel, out_shape=[jax.ShapeDtypeStruct((8, TOK), f32...]
where the time goes in v4:
time: 138 us; the launch traced here: 137 us
  Pallas kernels  133 us (96%)
  local copies, waits for them, and re-layouts  4.18 us (3%)
    pallas_call x1, Pallas kernels, step(): pl.pallas_call(step_kernel, out_shape=[jax.ShapeDtypeStruct((8, TOK), f32...  133 us
    squeeze x2, local copies, waits for them, and re-layouts, local(): return (loss[0], grads[0], grads[1])  4.18 us

profile of v4, /device:TPU:1, one launch (start us, length us, event | category | flops | bytes accessed | tf_op | source)
XLA Modules:
  0.0 137.5 jit_solution(287400067228868599)
XLA Ops:
  0.6 132.7 %step.1 = (f32[8,128]{1,0:T(8,128)}, f32[2,1024,256]{2,1,0:T(8,128)}) custom-call(bf16[128,1024]{1,0:T(8,128)(2,1)} %user_feat.1, bf16[128,1024]{1,0:T(8,128)(2,1)} %item_feat.1, bf16[256,1024]{1,0:T(8,128)(2,1)} %corpus_feat.1, bf16[1024,256]{1,0:T(8,128)(2,1)} %user_weight.1, bf16[1024,256]{1,0:T(8,128)(2,1)} %item_weight.1, s32[1,128]{1,0:T(1,128)} %bitcast.11, ...), custom_call_target="tpu_custom_call" | custom-call | tf_op jit(solution)/shard_map/step/pallas_call | solution.py:543
  133.3 1.2 slice_bitcast_fusion.2
  134.5 3.0 %slice_bitcast_fusion = (f32[1024,256]{1,0:T(8,128)}, f32[1024,256]{1,0:T(8,128)}) fusion(f32[2,1024,256]{2,1,0:T(8,128)} %get-tuple-element.6), kind=kLoop, calls=%fused_computation | loop fusion | bytes 4194304 | tf_op jit(solution)/shard_map/squeeze | solution.py:580

commit v5 on v4

--- a/solution.py
+++ b/solution.py
@@ -257,20 +257,34 @@
     def source(way, s):
         return (z + NZ - s) % NZ if way == 0 else (z + s) % NZ
 
-    def z_step(buf, s, send_sem, recv_sem, work=()):
-        work = list(work)
+    def corpus_step(s, work):
         for e in (0, 1):
             for way in (0, 1):
-                if s == 8 and e != way:
-                    continue
-                at = source(way, s)
-                arrived(buf.at[at, e], send_sem.at[way, s - 1, e], recv_sem.at[way, s - 1, e], z_peers[way])
-                if s < 7 or (s == 7 and e == way):
-                    z_send(buf, at, s + 1, e, way, send_sem, recv_sem)
+                if s < 8 or e == way:
+                    at = source(way, s)
+                    arrived(corp.at[at, e], zc_send.at[way, s - 1, e], zc_recv.at[way, s - 1, e], z_peers[way])
+                    if s < 7 or (s == 7 and e == way):
+                        z_send(corp, at, s + 1, e, way, zc_send, zc_recv)
                 if work:
                     work.pop(0)()
-        for piece in work:
-            piece()
+
+    def user_send(at, s, way):
+        block = gus.at[at, y_lo]
+        send(block, block, zu_send.at[way, s - 1], zu_recv.at[way, s - 1], z_peers[way])
+
+    def user_step(s):
+        for way in (0, 1) if s < 8 else (0,):
+            at = source(way, s)
+            block = gus.at[at, y_lo]
+            arrived(block, zu_send.at[way, s - 1], zu_recv.at[way, s - 1], z_peers[way])
+            if s < 7 or (s == 7 and way == 0):
+                user_send(at, s + 1, way)
+            send(block, block, yu_send.at[way, s], yu_recv.at[way, s], y_partner)
+
+    def users_handed(s):
+        for way in (0, 1) if 0 < s < 8 else (0,):
+            block = gus.at[source(way, s), 1 - y_lo]
+            arrived(block, yu_send.at[way, s], yu_recv.at[way, s], y_partner)
 
     for e in (0, 1):
         for way in (0, 1):
@@ -290,6 +304,9 @@
     user_low = unit.astype(bf16)
     cyc[group, 0] = user_low
     gus[z, y_lo] = user_low
+    for way in (0, 1):
+        user_send(z, 1, way)
+    send(gus.at[z, y_lo], gus.at[z, y_lo], yu_send.at[0, 0], yu_recv.at[0, 0], y_partner)
     loads[4].wait()
     unit, inverse = project(itf[...], iw[...])
     unit_i[...] = unit
@@ -300,7 +317,6 @@
     send(cyc.at[group], cyc.at[group], yh_send, yh_recv, y_far)
     for k in range(1, NX):
         send(cyc.at[group], cyc.at[group], x_send.at[0, k - 1], x_recv.at[0, k - 1], x_peers[k - 1])
-    send(gus.at[z, y_lo], gus.at[z, y_lo], yu_send, yu_recv, y_partner)
     send(cyc.at[group], cyc.at[group], c_send.at[0, 0], c_recv.at[0, 0], sibling)
 
     def group_of(far, k, other):
@@ -345,7 +361,8 @@
         if 5 <= s <= 7:
             work[0] = count_piece(12 * s - 60, 12 * s - 54)
             work[2] = count_piece(12 * s - 54, min(12 * s - 48, ND))
-        z_step(corp, s, zc_send, zc_recv, work)
+        corpus_step(s, work)
+        user_step(s)
         if s == 1:
             for k in range(1, ND):
                 send(codes.at[dev], codes.at[dev], codes_send.at[k - 1], codes_recv.at[k - 1], dev_peers[k - 1])
@@ -367,11 +384,6 @@
             for k in range(1, ND):
                 at = lax.rem(dev + ND - k, ND)
                 arrived(codes.at[at], codes_send.at[k - 1], codes_recv.at[k - 1], dev_peers[k - 1])
-        if s == 7:
-            arrived(gus.at[z, 1 - y_lo], yu_send, yu_recv, y_partner)
-            for e in (0, 1):
-                for way in (0, 1):
-                    z_send(gus, z, 1, e, way, zu_send, zu_recv)
     select[...] += select_from(source(0, 8))
     sel_out[...] = select[:, NEG:].astype(bf16)
     send(sel_out, sel_in, ys_send, ys_recv, y_partner)
@@ -427,7 +439,8 @@
 
     sums[...] = jnp.zeros((TOK, TOK), f32)
     own_sums[...] = jnp.zeros((TOK, TOK), f32)
-    z_step(gus, 1, zu_send, zu_recv, [forward_piece(n) for n in range(4)])
+    for n in range(NG // QUAD):
+        forward_piece(n)()
     arrived(sel_in, ys_send, ys_recv, y_partner)
     sample_low = (select[:, :NEG] + sel_in[...].astype(f32)).astype(bf16)
     sample_exp = jnp.exp(sharpen * dot(user_low, sample_low))
@@ -452,7 +465,8 @@
 
         return piece
 
-    z_step(gus, 2, zu_send, zu_recv, [user_piece(n) for n in range(4)])
+    for n in range(NG // QUAD):
+        user_piece(n)()
     user_back = unnormalize(unit_u[...], inv_u[...], upward[...])
 
     def user_part(n):
@@ -467,7 +481,8 @@
 
         return piece
 
-    z_step(gus, 3, zu_send, zu_recv, [user_parts(n) for n in range(4)])
+    for n in range(4):
+        user_parts(n)()
     for k in range(1, NG):
         arrived(tot_g.at[lax.rem(group + NG - k, NG)], tg_send.at[k - 1], tg_recv.at[k - 1], group_peers[k - 1])
 
@@ -482,10 +497,13 @@
 
         return piece
 
-    z_step(gus, 4, zu_send, zu_recv, [item_piece(n) for n in range(4)])
+    for n in range(NG // QUAD):
+        item_piece(n)()
     item_back = unnormalize(unit_i[...], inv_i[...], upward[...])
     mine[1] = dot(itf[...], item_back, 0, 0)
     on_core(0, reduce_first, 0)
+    for s in range(9):
+        users_handed(s)
     for k in range(1, ND):
         at = lax.rem(dev + ND - k, ND)
         arrived(tot_d.at[at], td_send.at[k - 1], td_recv.at[k - 1], dev_peers[k - 1])
@@ -509,14 +527,9 @@
     def both(s):
         return source(0, s), source(1, s)
 
-    z_step(gus, 5, zu_send, zu_recv, [corpus_piece(z, source(0, 1)), corpus_piece(source(1, 1), source(0, 2)),
-                                      corpus_piece(source(1, 2), source(0, 3)), corpus_piece(source(1, 3))])
-    on_core(0, reduce_second, 0)
-    z_step(gus, 6, zu_send, zu_recv, [corpus_piece(*both(4)), nothing, corpus_piece(*both(5)), nothing])
-    on_core(0, reduce_z, 0)
-    z_step(gus, 7, zu_send, zu_recv, [nothing, corpus_piece(*both(6))])
-    z_step(gus, 8, zu_send, zu_recv, [corpus_piece(*both(7))])
-    corpus_piece(source(0, 8))()
+    corpus_piece(z, source(0, 8))()
+    for s in range(1, 8):
+        corpus_piece(*both(s))()
     owned_back = (owned[...] - unit_c[...] * jnp.sum(unit_c[...] * owned[...], axis=-1, keepdims=True)) * inv_c[...]
     high = owned_back.astype(bf16)
     low = (owned_back - high.astype(f32)).astype(bf16)
@@ -529,6 +542,8 @@
     on_core(1, reduce_z, 1)
     on_core(1, gather_z, 1)
     on_core(1, gather_rest, 1)
+    on_core(0, reduce_second, 0)
+    on_core(0, reduce_z, 0)
     on_core(0, gather_z, 0)
     on_core(0, gather_rest, 0)
     on_core(1, take_gathered, 0)
@@ -543,7 +558,7 @@
     return pl.pallas_call(
         step_kernel,
         out_shape=[jax.ShapeDtypeStruct((8, TOK), f32), jax.ShapeDtypeStruct((2, WIDE, E), f32)],
-        in_specs=[pl.BlockSpec(memory_space=pl.ANY)] * 8,
+        in_specs=[pl.BlockSpec(memory_space=pltpu.HBM)] * 8,
         out_specs=[pl.BlockSpec(memory_space=pltpu.VMEM)] * 2,
         scratch_shapes=[
             vmem((TOK, WIDE), bf16), vmem((TOK, WIDE), bf16), vmem((OWN, WIDE), bf16),
@@ -559,7 +574,7 @@
             vmem((2, WIDE, E), f32), vmem((8, PART, E), f32), vmem((2, 3, PART, E), f32), vmem((2, 3, BIT, E), f32),
             vmem((NZ - 1, 8, 128), f32),
             dma((8,)), *pairs(NG - 1), *pairs(ND - 1), *pairs(), *pairs(NG - 1), *pairs(ND - 1),
-            *pairs(2, 8, 2), *pairs(2, 8, 2), *pairs(), *pairs(), *pairs(), *pairs(2, 3), *pairs(2, 4),
+            *pairs(2, 8, 2), *pairs(2, 8), *pairs(2, 9), *pairs(), *pairs(), *pairs(2, 3), *pairs(2, 4),
             *pairs(8), *pairs(2, 3), *pairs(2, 3), *pairs(NZ - 1), *pairs(NZ - 1), *pairs(2, 3), *pairs(2, 3),
             *pairs(2, 4),
         ],

time: 138 us -> 126 us (0.913)
  Pallas kernels: 133 us -> 121 us
    pallas_call x1, Pallas kernels: 133 us -> 121 us  [step(): pl.pallas_call(step_kernel, out_shape=[jax.ShapeDtypeStruct((8, TOK), f32...]
where the time goes in v5:
time: 126 us; the launch traced here: 125 us
  Pallas kernels  121 us (96%)
  local copies, waits for them, and re-layouts  4.18 us (3%)
    pallas_call x1, Pallas kernels, step(): pl.pallas_call(step_kernel, out_shape=[jax.ShapeDtypeStruct((8, TOK), f32...  121 us
    squeeze x2, local copies, waits for them, and re-layouts, local(): return (loss[0], grads[0], grads[1])  4.18 us

profile of v5, /device:TPU:1, one launch (start us, length us, event | category | flops | bytes accessed | tf_op | source)
XLA Modules:
  0.0 125.4 jit_solution(11312328275085273808)
XLA Ops:
  0.6 120.6 %step.1 = (f32[8,128]{1,0:T(8,128)}, f32[2,1024,256]{2,1,0:T(8,128)}) custom-call(bf16[128,1024]{1,0:T(8,128)(2,1)} %user_feat.1, bf16[128,1024]{1,0:T(8,128)(2,1)} %item_feat.1, bf16[256,1024]{1,0:T(8,128)(2,1)} %corpus_feat.1, bf16[1024,256]{1,0:T(8,128)(2,1)} %user_weight.1, bf16[1024,256]{1,0:T(8,128)(2,1)} %item_weight.1, s32[1,128]{1,0:T(1,128)} %bitcast.11, ...), custom_call_target="tpu_custom_call" | custom-call | tf_op jit(solution)/shard_map/step/pallas_call | solution.py:558
  121.2 1.2 slice_bitcast_fusion.2
  122.4 3.0 %slice_bitcast_fusion = (f32[1024,256]{1,0:T(8,128)}, f32[1024,256]{1,0:T(8,128)}) fusion(f32[2,1024,256]{2,1,0:T(8,128)} %get-tuple-element.6), kind=kLoop, calls=%fused_computation | loop fusion | bytes 4194304 | tf_op jit(solution)/shard_map/squeeze | solution.py:595

commit v6 on v5

--- a/solution.py
+++ b/solution.py
@@ -1,3 +1,5 @@
+import functools
+
 import jax
 import jax.numpy as jnp
 from jax import lax
@@ -67,7 +69,7 @@
     uf, itf, cf, uw, iw, ids_own, owner_own, row_own, corp, gus, cyc, ids, codes, pair_codes, tot_g, tot_d,
     select, sel_out, sel_in, cexp, counts, sums, own_sums, unit_u, unit_i, unit_c, inv_u, inv_i, inv_c, upward, owned,
     mine, from_core, from_first, from_second, from_z,
-    load_sem, ids_send, ids_recv, codes_send, codes_recv, pair_send, pair_recv, tg_send, tg_recv, td_send, td_recv,
+    load_sem, ids_send, ids_recv, zn_send, zn_recv, yn_send, yn_recv, pair_send, pair_recv, tg_send, tg_recv, td_send, td_recv,
     zc_send, zc_recv, zu_send, zu_recv, yu_send, yu_recv, ys_send, ys_recv,
     yh_send, yh_recv, x_send, x_recv, c_send, c_recv,
     core_send, core_recv, first_send, first_recv, second_send, second_recv, z_sends, z_recvs,
@@ -106,7 +108,7 @@
         remote(dst, dst, send_sem, recv_sem, device).wait_recv()
 
     barrier = pltpu.get_barrier_semaphore()
-    greeted = group_peers + dev_peers + [device_at(core, x, NY - 1 - y, z)]
+    greeted = [sibling] + x_peers + y_peers + z_peers
     for partner in greeted:
         pl.semaphore_signal(barrier, inc=1, device_id=partner, device_id_type=MESH)
 
@@ -271,20 +273,27 @@
     def user_send(at, s, way):
         block = gus.at[at, y_lo]
         send(block, block, zu_send.at[way, s - 1], zu_recv.at[way, s - 1], z_peers[way])
+        named = codes.at[at * 2 + y_lo]
+        send(named, named, zn_send.at[way, s - 1], zn_recv.at[way, s - 1], z_peers[way])
 
     def user_step(s):
         for way in (0, 1) if s < 8 else (0,):
             at = source(way, s)
             block = gus.at[at, y_lo]
+            named = codes.at[at * 2 + y_lo]
             arrived(block, zu_send.at[way, s - 1], zu_recv.at[way, s - 1], z_peers[way])
+            arrived(named, zn_send.at[way, s - 1], zn_recv.at[way, s - 1], z_peers[way])
             if s < 7 or (s == 7 and way == 0):
                 user_send(at, s + 1, way)
             send(block, block, yu_send.at[way, s], yu_recv.at[way, s], y_partner)
+            send(named, named, yn_send.at[way, s], yn_recv.at[way, s], y_partner)
 
     def users_handed(s):
         for way in (0, 1) if 0 < s < 8 else (0,):
             block = gus.at[source(way, s), 1 - y_lo]
+            named = codes.at[source(way, s) * 2 + 1 - y_lo]
             arrived(block, yu_send.at[way, s], yu_recv.at[way, s], y_partner)
+            arrived(named, yn_send.at[way, s], yn_recv.at[way, s], y_partner)
 
     for e in (0, 1):
         for way in (0, 1):
@@ -307,6 +316,7 @@
     for way in (0, 1):
         user_send(z, 1, way)
     send(gus.at[z, y_lo], gus.at[z, y_lo], yu_send.at[0, 0], yu_recv.at[0, 0], y_partner)
+    send(codes.at[dev], codes.at[dev], yn_send.at[0, 0], yn_recv.at[0, 0], y_partner)
     loads[4].wait()
     unit, inverse = project(itf[...], iw[...])
     unit_i[...] = unit
@@ -314,10 +324,25 @@
     item_low = unit.astype(bf16)
     cyc[group, 1] = item_low
     far_group = lax.rem(group + NG // 2, NG)
-    send(cyc.at[group], cyc.at[group], yh_send, yh_recv, y_far)
-    for k in range(1, NX):
-        send(cyc.at[group], cyc.at[group], x_send.at[0, k - 1], x_recv.at[0, k - 1], x_peers[k - 1])
-    send(cyc.at[group], cyc.at[group], c_send.at[0, 0], c_recv.at[0, 0], sibling)
+
+    def pass_block(at, kind, n, send_sem, recv_sem, device):
+        send(cyc.at[at], cyc.at[at], send_sem, recv_sem, device)
+        send(ids.at[at], ids.at[at], ids_send.at[kind, n], ids_recv.at[kind, n], device)
+
+    def block_arrived(at, kind, n, send_sem, recv_sem, device):
+        arrived(cyc.at[at], send_sem, recv_sem, device)
+        arrived(ids.at[at], ids_send.at[kind, n], ids_recv.at[kind, n], device)
+
+    def pass_along_x(at, far):
+        for k in range(1, NX):
+            pass_block(at, far, k, x_send.at[far, k - 1], x_recv.at[far, k - 1], x_peers[k - 1])
+
+    def pass_to_sibling(at, far, k):
+        pass_block(at, 2 + far, k, c_send.at[far, k], c_recv.at[far, k], sibling)
+
+    pass_block(group, 0, 0, yh_send, yh_recv, y_far)
+    pass_along_x(group, 0)
+    pass_to_sibling(group, 0, 0)
 
     def group_of(far, k, other):
         row = y_hi + far * (1 - 2 * y_hi)
@@ -346,53 +371,52 @@
     code_rows = lax.broadcasted_iota(jnp.int32, (OWN, NEG), 0) + dev * OWN
     ones = jnp.ones((NEG, 128), bf16)
 
-    def count_named(holder, carry):
+    def count_named(holder):
         named = codes[holder]
         row = jnp.concatenate([named[n : n + 1] for n in range(4)], axis=1)
         counts[holder] = dot((row == code_rows).astype(f32).astype(bf16), ones).astype(bf16)
-        return carry
-
-    def count_piece(first, last):
-        return lambda: lax.fori_loop(first, last, count_named, 0, unroll=2)
+
+    def count_piece(s, plane):
+        def piece():
+            for way in (0, 1) if 0 < s < 8 else (0,):
+                count_named(source(way, s) * 2 + plane)
+
+        return piece
+
+    def hand_and_count(s):
+        users_handed(s)
+        count_piece(s, 1 - y_lo)()
 
     select[...] = select_from(z)
+    count_piece(0, y_lo)()
     for s in range(1, 9):
         work = [nothing, select_more(0, s - 1), nothing, select_more(1, s - 1)] if s > 1 else []
-        if 5 <= s <= 7:
-            work[0] = count_piece(12 * s - 60, 12 * s - 54)
-            work[2] = count_piece(12 * s - 54, min(12 * s - 48, ND))
+        if s > 1:
+            work[0] = count_piece(s - 1, y_lo)
+        if s > 2:
+            work[2] = functools.partial(hand_and_count, s - 3)
         corpus_step(s, work)
         user_step(s)
-        if s == 1:
-            for k in range(1, ND):
-                send(codes.at[dev], codes.at[dev], codes_send.at[k - 1], codes_recv.at[k - 1], dev_peers[k - 1])
         if s == 2:
-            arrived(cyc.at[far_group], yh_send, yh_recv, y_far)
+            block_arrived(far_group, 0, 0, yh_send, yh_recv, y_far)
+            pass_along_x(far_group, 1)
+            pass_to_sibling(far_group, 1, 0)
+        if s in (5, 7):
+            far = (s - 5) // 2
             for k in range(1, NX):
-                send(cyc.at[far_group], cyc.at[far_group], x_send.at[1, k - 1], x_recv.at[1, k - 1], x_peers[k - 1])
-            send(cyc.at[far_group], cyc.at[far_group], c_send.at[1, 0], c_recv.at[1, 0], sibling)
-        if s == 3:
-            for k in range(1, NG):
-                send(ids.at[group], ids.at[group], ids_send.at[k - 1], ids_recv.at[k - 1], group_peers[k - 1])
-        if s in (4, 6):
-            far = (s - 4) // 2
-            for k in range(1, NX):
-                block = cyc.at[group_of(far, k, 0)]
-                arrived(block, x_send.at[far, k - 1], x_recv.at[far, k - 1], x_peers[k - 1])
-                send(block, block, c_send.at[far, k], c_recv.at[far, k], sibling)
-        if s == 4:
-            for k in range(1, ND):
-                at = lax.rem(dev + ND - k, ND)
-                arrived(codes.at[at], codes_send.at[k - 1], codes_recv.at[k - 1], dev_peers[k - 1])
+                at = group_of(far, k, 0)
+                block_arrived(at, far, k, x_send.at[far, k - 1], x_recv.at[far, k - 1], x_peers[k - 1])
+                pass_to_sibling(at, far, k)
     select[...] += select_from(source(0, 8))
     sel_out[...] = select[:, NEG:].astype(bf16)
     send(sel_out, sel_in, ys_send, ys_recv, y_partner)
 
+    count_piece(8, y_lo)()
+    for s in (6, 7, 8):
+        hand_and_count(s)
     for far in (0, 1):
         for k in range(NX):
-            arrived(cyc.at[group_of(far, k, 1)], c_send.at[far, k], c_recv.at[far, k], sibling)
-    for k in range(1, NG):
-        arrived(ids.at[lax.rem(group + NG - k, NG)], ids_send.at[k - 1], ids_recv.at[k - 1], group_peers[k - 1])
+            block_arrived(group_of(far, k, 1), 2 + far, k, c_send.at[far, k], c_recv.at[far, k], sibling)
 
     tile_rows = lax.broadcasted_iota(jnp.int32, (TOK, TOK), 0)
     tile_columns = lax.broadcasted_iota(jnp.int32, (TOK, TOK), 1)
@@ -502,8 +526,6 @@
     item_back = unnormalize(unit_i[...], inv_i[...], upward[...])
     mine[1] = dot(itf[...], item_back, 0, 0)
     on_core(0, reduce_first, 0)
-    for s in range(9):
-        users_handed(s)
     for k in range(1, ND):
         at = lax.rem(dev + ND - k, ND)
         arrived(tot_d.at[at], td_send.at[k - 1], td_recv.at[k - 1], dev_peers[k - 1])
@@ -573,7 +595,7 @@
             vmem((TOK, 1), f32), vmem((TOK, 1), f32), vmem((OWN, 1), f32), vmem((TOK, E), f32), vmem((OWN, E), f32),
             vmem((2, WIDE, E), f32), vmem((8, PART, E), f32), vmem((2, 3, PART, E), f32), vmem((2, 3, BIT, E), f32),
             vmem((NZ - 1, 8, 128), f32),
-            dma((8,)), *pairs(NG - 1), *pairs(ND - 1), *pairs(), *pairs(NG - 1), *pairs(ND - 1),
+            dma((8,)), *pairs(4, 4), *pairs(2, 8), *pairs(2, 9), *pairs(), *pairs(NG - 1), *pairs(ND - 1),
             *pairs(2, 8, 2), *pairs(2, 8), *pairs(2, 9), *pairs(), *pairs(), *pairs(2, 3), *pairs(2, 4),
             *pairs(8), *pairs(2, 3), *pairs(2, 3), *pairs(NZ - 1), *pairs(NZ - 1), *pairs(2, 3), *pairs(2, 3),
             *pairs(2, 4),

time: 126 us -> 120 us (0.952)
  Pallas kernels: 121 us -> 115 us
    pallas_call x1, Pallas kernels: 121 us -> 115 us  [step(): pl.pallas_call(step_kernel, out_shape=[jax.ShapeDtypeStruct((8, TOK), f32...]
where the time goes in v6:
time: 120 us; the launch traced here: 119 us
  Pallas kernels  115 us (96%)
  local copies, waits for them, and re-layouts  4.18 us (3%)
    pallas_call x1, Pallas kernels, step(): pl.pallas_call(step_kernel, out_shape=[jax.ShapeDtypeStruct((8, TOK), f32...  115 us
    squeeze x2, local copies, waits for them, and re-layouts, local(): return (loss[0], grads[0], grads[1])  4.18 us

profile of v6, /device:TPU:1, one launch (start us, length us, event | category | flops | bytes accessed | tf_op | source)
XLA Modules:
  0.0 119.5 jit_solution(17961835112882101676)
XLA Ops:
  0.6 114.6 %step.1 = (f32[8,128]{1,0:T(8,128)}, f32[2,1024,256]{2,1,0:T(8,128)}) custom-call(bf16[128,1024]{1,0:T(8,128)(2,1)} %user_feat.1, bf16[128,1024]{1,0:T(8,128)(2,1)} %item_feat.1, bf16[256,1024]{1,0:T(8,128)(2,1)} %corpus_feat.1, bf16[1024,256]{1,0:T(8,128)(2,1)} %user_weight.1, bf16[1024,256]{1,0:T(8,128)(2,1)} %item_weight.1, s32[1,128]{1,0:T(1,128)} %bitcast.11, ...), custom_call_target="tpu_custom_call" | custom-call | tf_op jit(solution)/shard_map/step/pallas_call | solution.py:580
  115.3 1.2 slice_bitcast_fusion.2
  116.5 3.0 %slice_bitcast_fusion = (f32[1024,256]{1,0:T(8,128)}, f32[1024,256]{1,0:T(8,128)}) fusion(f32[2,1024,256]{2,1,0:T(8,128)} %get-tuple-element.6), kind=kLoop, calls=%fused_computation | loop fusion | bytes 4194304 | tf_op jit(solution)/shard_map/squeeze | solution.py:617

commit v7 on v6

--- a/solution.py
+++ b/solution.py
@@ -477,7 +477,7 @@
     for k in range(1, NG):
         send(tot_g.at[group], tot_g.at[group], tg_send.at[k - 1], tg_recv.at[k - 1], group_peers[k - 1])
     own_logit = jnp.sum(own_sums[...], axis=1, keepdims=True)
-    loss_ref[...] = jnp.broadcast_to(to_row(jnp.log(total) - own_logit), (8, TOK))
+    loss_ref[...] = to_row(jnp.log(total) - own_logit)
     inverse_total = 1.0 / total
     sample_grad = (sample_exp * inverse_total * factor).astype(bf16)
 
@@ -579,7 +579,7 @@
     pairs = lambda *shape: [dma(shape), dma(shape)]
     return pl.pallas_call(
         step_kernel,
-        out_shape=[jax.ShapeDtypeStruct((8, TOK), f32), jax.ShapeDtypeStruct((2, WIDE, E), f32)],
+        out_shape=[jax.ShapeDtypeStruct((1, TOK), f32), jax.ShapeDtypeStruct((2, WIDE, E), f32)],
         in_specs=[pl.BlockSpec(memory_space=pltpu.HBM)] * 8,
         out_specs=[pl.BlockSpec(memory_space=pltpu.VMEM)] * 2,
         scratch_shapes=[
@@ -614,7 +614,7 @@
         user_feat, item_feat, corpus_feat, user_weight, item_weight,
         item_ids.reshape(1, TOK), neg_owner.reshape(4, 128), neg_row.reshape(4, 128),
     )
-    return loss[0], grads[0], grads[1]
+    return loss.reshape(TOK), grads[0], grads[1]
 
 
 def solution(mesh):

time: 120 us -> 119 us (level)
    squeeze x2 -> x1, local copies, waits for them, and re-layouts: 4.18 us -> 2.99 us  [local(): return (loss.reshape(TOK), grads[0], grads[1])]
where the time goes in v7:
time: 119 us
  Pallas kernels  115 us (97%)
  local copies, waits for them, and re-layouts  3.51 us (3%)
    pallas_call x1, Pallas kernels, step(): pl.pallas_call(step_kernel, out_shape=[jax.ShapeDtypeStruct((1, TOK), f32...  115 us
    squeeze x1, local copies, waits for them, and re-layouts, local(): return (loss.reshape(TOK), grads[0], grads[1])  2.99 us

profile of v7, /device:TPU:1, one launch (start us, length us, event | category | flops | bytes accessed | tf_op | source)
XLA Modules:
  0.0 118.8 jit_solution(10307332159883112911)
XLA Ops:
  0.6 114.6 %step.1 = (f32[1,128]{1,0:T(1,128)}, f32[2,1024,256]{2,1,0:T(8,128)}) custom-call(bf16[128,1024]{1,0:T(8,128)(2,1)} %user_feat.1, bf16[128,1024]{1,0:T(8,128)(2,1)} %item_feat.1, bf16[256,1024]{1,0:T(8,128)(2,1)} %corpus_feat.1, bf16[1024,256]{1,0:T(8,128)(2,1)} %user_weight.1, bf16[1024,256]{1,0:T(8,128)(2,1)} %item_weight.1, s32[1,128]{1,0:T(1,128)} %bitcast.10, ...), custom_call_target="tpu_custom_call" | custom-call | tf_op jit(solution)/shard_map/step/pallas_call | solution.py:580
  115.3 0.0 copy-start
  115.3 3.0 %slice_bitcast_fusion = (f32[1024,256]{1,0:T(8,128)}, f32[1024,256]{1,0:T(8,128)}) fusion(f32[2,1024,256]{2,1,0:T(8,128)} %get-tuple-element.6), kind=kLoop, calls=%fused_computation | loop fusion | bytes 4194304 | tf_op jit(solution)/shard_map/squeeze | solution.py:617
  118.3 0.0 copy-done
  118.3 0.5 copy.12
Async XLA Ops:
  115.3 3.0 %copy-start = (f32[1,128]{1,0:T(1,128)S(1)}, f32[1,128]{1,0:T(1,128)}, u32[]{:S(2)}) copy-start(f32[1,128]{1,0:T(1,128)} %get-tuple-element.5) | copy-start | bytes 1540
